TPU v7x, 32 devices: a whole 2x2x4 slice. The times are simulated.
32 devices in a mesh: dp: 8 (over y, x, core), tp: 4 (over z).
Axes of the slice: x: 2, y: 2, z: 4, core: 2. Of those that a mesh axis runs over, the one named last changes fastest.
Arguments:
- tokens: bfloat16 [16384, 768], P('dp'), may hold values from -6 to 6
- segment_ids: int32 [32, 512], P('dp'), may hold values from 0 to 7, never falling along the last dimension, each value on 1 to 256 neighbouring positions
- pair_order: int32 [256], replicated, may hold values from 0 to 255, each once
- w_query: bfloat16 [768, 768], P(None, 'tp'), may hold values from -0.0546875 to 0.0546875
- w_key: bfloat16 [768, 768], P(None, 'tp'), may hold values from -0.21875 to 0.21875
- w_value: bfloat16 [768, 768], P(None, 'tp'), may hold values from -0.21875 to 0.21875
- w_out: bfloat16 [768, 768], P('tp'), may hold values from -0.625 to 0.625
- rel_bias: float32 [32, 12], P(None, 'tp'), may hold values from -4 to 4
- gain_attn: float32 [768], replicated, may hold values from 0.5 to 1.5
- w_hidden: bfloat16 [768, 3072], P(None, 'tp'), may hold values from -0.21875 to 0.21875
- w_down: bfloat16 [3072, 768], P('tp'), may hold values from -0.109375 to 0.109375
- gain_ffn: float32 [768], replicated, may hold values from 0.5 to 1.5
- gain_final: float32 [768], replicated, may hold values from 0.5 to 1.5
- w_project: bfloat16 [768, 768], replicated, may hold values from -0.21875 to 0.21875
Outputs:
- layer_out: bfloat16 [16384, 768], P('dp')
- d_tokens: float32 [16384, 768], P('dp')
- grad_query: float32 [768, 768], P('dp', 'tp')
- grad_key: float32 [768, 768], P('dp', 'tp')
- grad_value: float32 [768, 768], P('dp', 'tp')
- grad_out: float32 [768, 768], P('tp', 'dp')
- grad_rel_bias: float32 [32, 12], P(None, 'tp')
- grad_gain_attn: float32 [768], P('dp')
- grad_hidden: float32 [768, 3072], P('dp', 'tp')
- grad_down: float32 [3072, 768], P('tp', 'dp')
- grad_gain_ffn: float32 [768], P('dp')
- grad_gain_final: float32 [768], P('dp')
- grad_project: float32 [768, 768], P('dp')
Inputs may be any that keep to these rules, and one draw needn't show every extreme that they name: `segment_ids`: within each row the segment numbers never fall, and every number from 0 to 7 appears. `pair_order`: every number appears once.
All inputs are finite; a program needn't handle non-finite values.
Results may differ from a plain program's by a relative error of at most 0.034.
Values may be sent and summed in bfloat16 or wider, within the bound.
No kernel may reach another device: no remote copies, remote signals or barrier semaphores. Data moves between devices by JAX's collectives and lax.ppermute only.
A program may use at most 192 MiB of HBM per device.

v0:
```python
import math

import jax
import jax.numpy as jnp
import numpy as np
from jax import lax
from jax.sharding import PartitionSpec as P

MAX_DIST = 128
SEG_ROW = 8


epsilon = 1e-06
logit_scale = 50.0
loss_scale = 128.0
masked_value = -1e30
highest = lax.Precision.HIGHEST


def bucket_table(length, bucket_count, distance):
    half_count = bucket_count // 2
    exact_count = half_count // 2
    offsets = np.arange(length)[None, :] - np.arange(length)[:, None]
    far_side = np.where(offsets > 0, half_count, 0)
    magnitude = np.abs(offsets)
    logged = (
        np.log(np.maximum(magnitude, exact_count) / exact_count)
        / math.log(distance / exact_count)
        * (half_count - exact_count)
    )
    far_bucket = np.minimum(exact_count + logged.astype(np.int64), half_count - 1)
    return (far_side + np.where(magnitude < exact_count, magnitude, far_bucket)).astype(np.int32)


def normed(values, gain_vec):
    scaling = lax.rsqrt(jnp.mean(values * values, -1, keepdims=True) + epsilon)
    return (values * scaling * gain_vec, scaling)


def norm_back(grad_out, values, scaling, gain_vec):
    unit_vals = values * scaling
    weighted = grad_out * gain_vec
    d_input = scaling * (weighted - unit_vals * jnp.mean(weighted * unit_vals, -1, keepdims=True))
    return (d_input, jnp.sum(grad_out * unit_vals, 0))


def smooth_gate(values):
    return jax.nn.gelu(values, approximate=True)


def row_scores(queries, key_vecs, seg_row, rel_field):
    scores = (
        jnp.einsum("ihc,jhc->hij", queries, key_vecs, preferred_element_type=jnp.float32)
        + rel_field
    )
    same_seg = seg_row[:, None] == seg_row[None, :]
    return jnp.where(same_seg[None], scores, masked_value)


def attend(queries, key_vecs, val_vecs, seg_row, rel_field):
    scores = row_scores(queries, key_vecs, seg_row, rel_field)
    row_max = jnp.max(scores, -1, keepdims=True)
    log_total = row_max + jnp.log(jnp.sum(jnp.exp(scores - row_max), -1, keepdims=True))
    probs = jnp.exp(scores - log_total).astype(jnp.bfloat16)
    context = jnp.einsum("hij,jhc->ihc", probs, val_vecs, preferred_element_type=jnp.float32)
    return (context.astype(jnp.bfloat16), log_total)


def attend_back(queries, key_vecs, val_vecs, seg_row, log_total, d_context, rel_field):
    scores = row_scores(queries, key_vecs, seg_row, rel_field)
    prob_full = jnp.exp(scores - log_total)
    prob_low = prob_full.astype(jnp.bfloat16)
    d_probs = jnp.einsum("ihc,jhc->hij", d_context, val_vecs, preferred_element_type=jnp.float32)
    d_vals = jnp.einsum("hij,ihc->jhc", prob_low, d_context, preferred_element_type=jnp.float32)
    row_delta = jnp.sum(prob_full * d_probs, -1, keepdims=True)
    d_scores = (prob_full * (d_probs - row_delta)).astype(jnp.bfloat16)
    d_queries = jnp.einsum("hij,jhc->ihc", d_scores, key_vecs, preferred_element_type=jnp.float32)
    d_keys = jnp.einsum("hij,ihc->jhc", d_scores, queries, preferred_element_type=jnp.float32)
    return (
        d_queries.astype(jnp.bfloat16),
        d_keys.astype(jnp.bfloat16),
        d_vals.astype(jnp.bfloat16),
        d_scores,
    )


def shards(
    tokens,
    segment_ids,
    pair_order,
    w_query,
    w_key,
    w_value,
    w_out,
    rel_bias,
    gain_attn,
    w_hidden,
    w_down,
    gain_ffn,
    gain_final,
    w_project,
):
    row_count, length = segment_ids.shape
    bucket_count, heads_here = rel_bias.shape
    head_dim = w_query.shape[1] // heads_here
    token_count = row_count * length
    head_shape = (row_count, length, heads_here, head_dim)
    bucket_ids = jnp.asarray(bucket_table(length, bucket_count, MAX_DIST))
    bucket_hot = (bucket_ids[None] == jnp.arange(bucket_count)[:, None, None]).astype(jnp.float32)
    rel_field = jnp.einsum("bij,bh->hij", bucket_hot, rel_bias, precision=highest)
    x_in = tokens.astype(jnp.float32)
    normed_one, scale_one = normed(x_in, gain_attn)
    normed_one = normed_one.astype(jnp.bfloat16)
    queries = (
        jnp.dot(normed_one, w_query, preferred_element_type=jnp.float32)
        .astype(jnp.bfloat16)
        .reshape(head_shape)
    )
    key_vecs = (
        jnp.dot(normed_one, w_key, preferred_element_type=jnp.float32)
        .astype(jnp.bfloat16)
        .reshape(head_shape)
    )
    val_vecs = (
        jnp.dot(normed_one, w_value, preferred_element_type=jnp.float32)
        .astype(jnp.bfloat16)
        .reshape(head_shape)
    )

    def forward_row(inputs):
        return attend(inputs[0], inputs[1], inputs[2], inputs[3], rel_field)

    context, log_totals = lax.map(forward_row, (queries, key_vecs, val_vecs, segment_ids))
    context = context.reshape(token_count, heads_here * head_dim)
    attn_part = jnp.dot(context, w_out, preferred_element_type=jnp.float32).astype(jnp.bfloat16)
    middle = x_in + lax.psum(attn_part, "tp").astype(jnp.float32)
    normed_two, scale_two = normed(middle, gain_ffn)
    normed_two = normed_two.astype(jnp.bfloat16)
    pre_act = jnp.dot(normed_two, w_hidden, preferred_element_type=jnp.float32)
    hidden = smooth_gate(pre_act).astype(jnp.bfloat16)
    ffn_part = jnp.dot(hidden, w_down, preferred_element_type=jnp.float32).astype(jnp.bfloat16)
    result = middle + lax.psum(ffn_part, "tp").astype(jnp.float32)
    final, scale_end = normed(result, gain_final)
    layer_out = final.astype(jnp.bfloat16)
    slots_here = row_count * SEG_ROW
    slot_of = (segment_ids + SEG_ROW * jnp.arange(row_count, dtype=jnp.int32)[:, None]).reshape(
        token_count
    )
    member = (slot_of[None, :] == jnp.arange(slots_here, dtype=jnp.int32)[:, None]).astype(
        jnp.float32
    )
    counts = jnp.sum(member, 1, keepdims=True)
    pooled = jnp.dot(member, final, precision=highest) / counts
    pooled_low = pooled.astype(jnp.bfloat16)
    projected = jnp.dot(pooled_low, w_project, preferred_element_type=jnp.float32)
    inv_norm = lax.rsqrt(jnp.sum(projected * projected, -1, keepdims=True) + epsilon)
    unit_vec = projected * inv_norm
    embedded = unit_vec.astype(jnp.bfloat16)
    emb_all = lax.all_gather(embedded, "dp", axis=0, tiled=True)
    slot_total = emb_all.shape[0]
    start_slot = lax.axis_index("dp") * slots_here
    own_slots = start_slot + jnp.arange(slots_here, dtype=jnp.int32)
    all_slots = jnp.arange(slot_total, dtype=jnp.int32)
    self_mask = own_slots[:, None] == all_slots[None, :]
    similar = logit_scale * jnp.einsum(
        "sd,nd->sn", embedded, emb_all, preferred_element_type=jnp.float32
    )
    similar = jnp.where(self_mask, masked_value, similar)
    pair_all = pair_order // 2
    pair_here = lax.dynamic_slice_in_dim(pair_all, start_slot, slots_here)
    target = jnp.where(
        (pair_here[:, None] == pair_all[None, :]) & jnp.logical_not(self_mask), 1.0, 0.0
    )
    row_max = jnp.max(similar, -1, keepdims=True)
    log_total = row_max + jnp.log(jnp.sum(jnp.exp(similar - row_max), -1, keepdims=True))
    row_prob = jnp.exp(similar - log_total)
    emb_all_full = emb_all.astype(jnp.float32)
    row_grad = loss_scale * logit_scale * (row_prob - target)
    own_part = jnp.dot(row_grad, emb_all_full, precision=highest)
    spread = jnp.einsum("sn,sd->nd", row_grad, embedded.astype(jnp.float32), precision=highest)
    d_unit = own_part + lax.psum_scatter(spread, "dp", scatter_dimension=0, tiled=True)
    d_proj = (
        inv_norm * (d_unit - unit_vec * jnp.sum(d_unit * unit_vec, -1, keepdims=True))
    ).astype(jnp.bfloat16)
    d_project = jnp.einsum("sd,se->de", pooled_low, d_proj, preferred_element_type=jnp.float32)
    d_pooled = jnp.einsum("se,de->sd", d_proj, w_project, preferred_element_type=jnp.float32)
    d_final = jnp.einsum("st,sd->td", member, d_pooled / counts, precision=highest)
    d_result, d_gain_end = norm_back(d_final, result, scale_end, gain_final)
    d_ffn = d_result.astype(jnp.bfloat16)
    d_down = jnp.einsum("tf,td->fd", hidden, d_ffn, preferred_element_type=jnp.float32)
    d_hid = jnp.einsum("td,fd->tf", d_ffn, w_down, preferred_element_type=jnp.float32)
    unused_gate, gate_back = jax.vjp(smooth_gate, pre_act)
    d_pre = gate_back(d_hid)[0].astype(jnp.bfloat16)
    d_hidden_w = jnp.einsum("td,tf->df", normed_two, d_pre, preferred_element_type=jnp.float32)
    d_normed_two = lax.psum(
        jnp.einsum("tf,df->td", d_pre, w_hidden, preferred_element_type=jnp.float32).astype(
            jnp.bfloat16
        ),
        "tp",
    ).astype(jnp.float32)
    d_mid_norm, d_gain_two = norm_back(d_normed_two, middle, scale_two, gain_ffn)
    d_middle = d_result + d_mid_norm
    d_attn = d_middle.astype(jnp.bfloat16)
    d_out_w = jnp.einsum("tk,td->kd", context, d_attn, preferred_element_type=jnp.float32)
    d_context = (
        jnp.einsum("td,kd->tk", d_attn, w_out, preferred_element_type=jnp.float32)
        .astype(jnp.bfloat16)
        .reshape(head_shape)
    )

    def backward_row(carry, inputs):
        d_q, d_k, d_v, d_s = attend_back(
            inputs[0], inputs[1], inputs[2], inputs[3], inputs[4], inputs[5], rel_field
        )
        return (carry + d_s.astype(jnp.float32), (d_q, d_k, d_v))

    d_field, (d_queries, d_keys, d_vals) = lax.scan(
        backward_row,
        jnp.zeros((heads_here, length, length), jnp.float32),
        (queries, key_vecs, val_vecs, segment_ids, log_totals, d_context),
    )
    d_rel_part = jnp.einsum("bij,hij->bh", bucket_hot, d_field, precision=highest)
    flat_cols = heads_here * head_dim
    d_queries = d_queries.reshape(token_count, flat_cols)
    d_keys = d_keys.reshape(token_count, flat_cols)
    d_vals = d_vals.reshape(token_count, flat_cols)
    d_query_w = jnp.einsum("td,tk->dk", normed_one, d_queries, preferred_element_type=jnp.float32)
    d_key_w = jnp.einsum("td,tk->dk", normed_one, d_keys, preferred_element_type=jnp.float32)
    d_value_w = jnp.einsum("td,tk->dk", normed_one, d_vals, preferred_element_type=jnp.float32)
    d_normed_part = jnp.einsum("tk,dk->td", d_queries, w_query, preferred_element_type=jnp.float32)
    d_normed_part = d_normed_part + jnp.einsum(
        "tk,dk->td", d_keys, w_key, preferred_element_type=jnp.float32
    )
    d_normed_part = d_normed_part + jnp.einsum(
        "tk,dk->td", d_vals, w_value, preferred_element_type=jnp.float32
    )
    d_normed_one = lax.psum(d_normed_part.astype(jnp.bfloat16), "tp").astype(jnp.float32)
    d_in_norm, d_gain_one = norm_back(d_normed_one, x_in, scale_one, gain_attn)
    d_tokens = d_middle + d_in_norm
    grads = (
        lax.psum_scatter(d_query_w, "dp", scatter_dimension=0, tiled=True),
        lax.psum_scatter(d_key_w, "dp", scatter_dimension=0, tiled=True),
        lax.psum_scatter(d_value_w, "dp", scatter_dimension=0, tiled=True),
        lax.psum_scatter(d_out_w, "dp", scatter_dimension=1, tiled=True),
        lax.psum_scatter(d_hidden_w, "dp", scatter_dimension=0, tiled=True),
        lax.psum_scatter(d_down, "dp", scatter_dimension=1, tiled=True),
        lax.psum_scatter(d_project, "dp", scatter_dimension=0, tiled=True),
        lax.psum_scatter(d_gain_one, "dp", scatter_dimension=0, tiled=True),
        lax.psum_scatter(d_gain_two, "dp", scatter_dimension=0, tiled=True),
        lax.psum_scatter(d_gain_end, "dp", scatter_dimension=0, tiled=True),
    )
    d_rel = lax.psum(d_rel_part, "dp")
    return (
        layer_out,
        d_tokens,
        grads[0],
        grads[1],
        grads[2],
        grads[3],
        d_rel,
        grads[7],
        grads[4],
        grads[5],
        grads[8],
        grads[9],
        grads[6],
    )


def solution(mesh):
    placed = (
        P("dp", None),
        P("dp", None),
        P(),
        P(None, "tp"),
        P(None, "tp"),
        P(None, "tp"),
        P("tp", None),
        P(None, "tp"),
        P(),
        P(None, "tp"),
        P("tp", None),
        P(),
        P(),
        P(),
    )
    return jax.shard_map(
        shards,
        mesh=mesh,
        in_specs=placed,
        out_specs=(
            P("dp", None),
            P("dp", None),
            P("dp", "tp"),
            P("dp", "tp"),
            P("dp", "tp"),
            P("tp", "dp"),
            P(None, "tp"),
            P("dp"),
            P("dp", "tp"),
            P("tp", "dp"),
            P("dp"),
            P("dp"),
            P("dp", None),
        ),
        check_vma=False,
    )
```

profile of v0, /device:TPU:0, one launch (start us, length us, event | category | flops | bytes accessed | tf_op | source)
XLA Modules:
  0.0 1003.2 jit_solution(5088652044670015031)
XLA Ops:
  25.9 12.7 %fusion.82 = f32[3,512,512]{2,0,1:T(4,128)} fusion(s32[512,512]{1,0:T(8,128)} %constant.107.clone, f32[32,3]{0,1:T(4,128)S(1)} %copy-done.45), kind=kOutput, calls=%fused_computation.118 | convolution fusion | flops 310378496 | bytes 4194688 | tf_op jit(solution)/shard_map/bij,bh->hij/dot_general | solution.py:110
  38.6 4.9 copy.85
  44.5 21.0 %while.29 = (s32[]{:T(128)}, bf16[4,512,3,64]{1,3,2,0:T(8,128)(2,1)}, f32[4,3,512,1]{2,1,3,0:T(4,128)}, bf16[4,512,3,64]{1,3,2,0:T(8,128)(2,1)S(1)}, s32[4,512]{...) while((s32[]{:T(128)}, ...), condition=%wide.region_4.5_spmd, body=%wide.region_1.4_spmd.sunk | while | flops 207190528 | bytes 13955181 | solution.py:133
  71.4 123.9 %all-reduce.9.cloned.1.call-done = bf16[2048,768]{1,0:T(8,128)(2,1)} async-done(((bf16[2048,768]{1,0:T(8,128)(2,1)}), bf16[2048,768]{1,0:T(8,128)(2,1)}) %all-reduce.9.cloned.1.call-update) | async-done | bytes 3145744 | tf_op jit(solution)/shard_map/psum | solution.py:136
  195.3 4.1 multiply_reduce_fusion.4
  200.0 4.4 fusion.111
  207.1 5.4 convolution_convert_fusion.3
  215.1 117.7 %all-reduce.11.cloned.1.call-done = bf16[2048,768]{1,0:T(8,128)(2,1)} async-done(((bf16[2048,768]{1,0:T(8,128)(2,1)}), bf16[2048,768]{1,0:T(8,128)(2,1)}) %all-reduce.11.cloned.1.call-update) | async-done | bytes 3145744 | tf_op jit(solution)/shard_map/psum | solution.py:142
  332.8 5.3 multiply_reduce_fusion.3
  344.7 9.5 all_gather.3
  358.0 33.2 %reduce-scatter.11.cloned.1.call-done = f32[32,768]{1,0:T(8,128)} async-done(((f32[256,768]{1,0:T(8,128)}), f32[32,768]{1,0:T(8,128)}) %reduce-scatter.11.cloned.1.call-update) | async-done | bytes 98320 | tf_op jit(solution)/shard_map/reduce_scatter | solution.py:181
  396.5 7.7 multiply_reduce_fusion.1
  406.9 6.1 fusion.71
  414.7 4.1 convolution_convert_fusion.2
  418.9 121.2 %all-reduce.13.cloned.1.call-done = bf16[2048,768]{1,0:T(8,128)(2,1)} async-done(((bf16[2048,768]{1,0:T(8,128)(2,1)}), bf16[2048,768]{1,0:T(8,128)(2,1)}) %all-reduce.13.cloned.1.call-update) | async-done | bytes 3145744 | tf_op jit(solution)/shard_map/psum | solution.py:195
  540.1 5.3 fusion.64
  545.5 5.7 fusion.63
  562.9 47.6 %while.30 = (s32[]{:T(128)}, f32[3,512,512]{1,2,0:T(8,128)}, bf16[4,512,3,64]{1,3,2,0:T(8,128)(2,1)}, bf16[4,512,3,64]{1,3,2,0:T(8,128)(2,1)}, bf16[4,512,3,64]{...) while((s32[]{:T(128)}, f32[3,512,512]{1,2,0:T(8,128)}, ...), condition=%wide.region_20.21_spmd.clone, body=%wide.region_18.20_spmd.clone.sunk | while | flops 513309184 | bytes 60730580 | solution.py:217
  622.6 9.6 fusion.86
  632.2 8.1 fusion.110
  649.6 5.2 copy.95
  658.7 17.7 %fusion.102 = f32[32,3]{0,1:T(4,128)S(1)} fusion(f32[3,512,512]{2,0,1:T(4,128)} %copy.95, s32[512,512]{1,0:T(8,128)S(1)} %copy-done.46), kind=kOutput, calls=%fused_computation.133 | convolution fusion | flops 310378496 | bytes 4194688 | tf_op jit(solution)/shard_map/bij,hij->bh/dot_general | solution.py:222
  678.0 62.5 %all-reduce.15.cloned.1.call-done = bf16[2048,768]{1,0:T(8,128)(2,1)} async-done(((bf16[2048,768]{1,0:T(8,128)(2,1)}), bf16[2048,768]{1,0:T(8,128)(2,1)}) %all-reduce.15.cloned.1.call-update) | async-done | bytes 3145744 | tf_op jit(solution)/shard_map/psum | solution.py:237
  740.5 4.2 fusion.74
  744.8 24.1 %all-reduce.3 = (f32[32,3]{0,1:T(4,128)}, f32[768]{0:T(1024)S(1)}, f32[768]{0:T(1024)S(1)}, f32[768]{0:T(1024)S(1)}) all-reduce(f32[32,3]{0,1:T(4,128)S(1)} %fusion.102, f32[768]{0:T(1024)S(1)} %get-tuple-element.250, f32[768]{0:T(1024)S(1)} %get-tuple-element.248, f32[768]{0:T(1024)S(1)} %copy-done.34), channel_id=1, replica_groups=mesh['dp'=8,'tp'=4] {'dp'}, use_global_device_ids=true, to_apply=%region_27.28 | all-reduce | flops 2400 | bytes 19200 | tf_op jit(solution)/shard_map/psum | solution.py:252
  770.6 7.5 fusion.60
  778.1 7.9 reduce-scatter.23.cloned.1.call-done
  786.0 46.8 %reduce-scatter.21.cloned.1.call-done = f32[768,96]{0,1:T(8,128)} async-done(((f32[768,768]{0,1:T(8,128)}), f32[768,96]{0,1:T(8,128)}) %reduce-scatter.21.cloned.1.call-update) | async-done | bytes 294928 | tf_op jit(solution)/shard_map/reduce_scatter | solution.py:246
  832.8 46.5 %reduce-scatter.19.cloned.1.call-done = f32[96,768]{1,0:T(8,128)} async-done(((f32[768,768]{1,0:T(8,128)}), f32[96,768]{1,0:T(8,128)}) %reduce-scatter.19.cloned.1.call-update) | async-done | bytes 294928 | tf_op jit(solution)/shard_map/reduce_scatter | solution.py:245
  879.2 38.9 %reduce-scatter.17.cloned.1.call-done = f32[96,192]{1,0:T(8,128)} async-done(((f32[768,192]{1,0:T(8,128)}), f32[96,192]{1,0:T(8,128)}) %reduce-scatter.17.cloned.1.call-update) | async-done | bytes 73744 | tf_op jit(solution)/shard_map/reduce_scatter | solution.py:243
  918.1 39.0 %reduce-scatter.13.cloned.1.call-done = f32[96,192]{1,0:T(8,128)} async-done(((f32[768,192]{1,0:T(8,128)}), f32[96,192]{1,0:T(8,128)}) %reduce-scatter.13.cloned.1.call-update) | async-done | bytes 73744 | tf_op jit(solution)/shard_map/reduce_scatter | solution.py:241
  957.2 38.9 %reduce-scatter.15.cloned.1.call-done = f32[96,192]{1,0:T(8,128)} async-done(((f32[768,192]{1,0:T(8,128)}), f32[96,192]{1,0:T(8,128)}) %reduce-scatter.15.cloned.1.call-update) | async-done | bytes 73744 | tf_op jit(solution)/shard_map/reduce_scatter | solution.py:242
  (274 shorter events, 158.9 us)
Async XLA Ops:
  7.2 200.0 %copy-start = (bf16[768,768]{1,0:T(8,128)(2,1)S(1)}, bf16[768,768]{1,0:T(8,128)(2,1)}, u32[]{:S(2)}) copy-start(bf16[768,768]{1,0:T(8,128)(2,1)} %param.29) | copy-start | bytes 3538948
  7.2 188.1 %all-reduce.9.cloned.1.call-start = ((), (), s32[]{:S(2)}) async-start(), calls=%async_computation.8 | async-start | bytes 6291456 | tf_op jit(solution)/shard_map/psum | solution.py:136
  71.3 128.7 %copy-start.35 = (f32[768]{0:T(1024)S(1)}, f32[768]{0:T(1024)}, u32[]{:S(2)}) copy-start(f32[768]{0:T(1024)} %param.30) | copy-start | bytes 9220
  71.4 261.4 %all-reduce.11.cloned.1.call-start = ((), (), s32[]{:S(2)}) async-start(), calls=%async_computation.9 | async-start | bytes 6291456 | tf_op jit(solution)/shard_map/psum | solution.py:142
  212.5 178.8 %reduce-scatter.11.cloned.1.call-start = ((), (), s32[]{:S(2)}) async-start(), calls=%async_computation.10 | async-start | bytes 884736 | tf_op jit(solution)/shard_map/reduce_scatter | solution.py:181
  213.4 124.7 %copy-start.37 = (s32[256]{0:T(256)}, s32[256]{0:T(256)S(1)}, u32[]{:S(2)}) copy-start(s32[256]{0:T(256)S(1)} %and_select_fusion) | copy-start | bytes 3076
  332.8 8.0 copy-start.32
  332.8 8.0 copy-start.39
  338.1 16.9 %copy-start.41 = (s32[32]{0:T(128)S(1)}, s32[32]{0:T(128)}, u32[]{:S(2)}) copy-start(s32[32]{0:T(128)} %iota_add_fusion) | copy-start | bytes 388
  338.1 18.4 %copy-start.42 = (s32[32]{0:T(128)S(1)}, s32[32]{0:T(128)}, u32[]{:S(2)}) copy-start(s32[32]{0:T(128)} %dynamic_slice.36) | copy-start | bytes 388
  338.1 18.4 %copy-start.38 = (s32[256]{0:T(256)S(1)}, s32[256]{0:T(256)}, u32[]{:S(2)}) copy-start(s32[256]{0:T(256)} %copy-done.37) | copy-start | bytes 3076
  344.0 11.3 %copy-start.14 = (f32[32,768]{1,0:T(8,128)}, f32[32,768]{1,0:T(8,128)S(1)}, u32[]{:S(2)}) copy-start(f32[32,768]{1,0:T(8,128)S(1)} %get-tuple-element.309) | copy-start | bytes 294916
  358.0 182.1 %all-reduce.13.cloned.1.call-start = ((), (), s32[]{:S(2)}) async-start(), calls=%async_computation.11 | async-start | bytes 6291456 | tf_op jit(solution)/shard_map/psum | solution.py:195
  394.5 9.6 slice-start
  396.5 10.5 %slice-start.2 = ((s8[6291456]{0:T(1024)(128)(4,1)}), s8[4194304]{0:T(1024)(128)(4,1)S(1)}, s32[]{:S(2)}) async-start(s8[6291456]{0:T(1024)(128)(4,1)} %bitcast.209), calls=%async_computation.22 | async-start | bytes 8388608
  406.9 7.8 copy-start.44
  414.7 125.4 %copy-start.30 = (f32[2048]{0:T(1024)S(1)}, f32[2048]{0:T(1024)}, u32[]{:S(2)}) copy-start(f32[2048]{0:T(1024)} %copy-done.29) | copy-start | bytes 24580
  414.7 125.4 %copy-start.36 = (f32[768]{0:T(1024)S(1)}, f32[768]{0:T(1024)}, u32[]{:S(2)}) copy-start(f32[768]{0:T(1024)} %param.30) | copy-start | bytes 9220
  418.9 257.5 %reduce-scatter.25.cloned.1.call-start = ((), (), s32[]{:S(2)}) async-start(), calls=%async_computation.19 | async-start | bytes 884736
  560.1 180.4 %all-reduce.15.cloned.1.call-start = ((), (), s32[]{:S(2)}) async-start(), calls=%async_computation.12 | async-start | bytes 6291456 | tf_op jit(solution)/shard_map/psum | solution.py:237
  620.3 165.7 %reduce-scatter.23.cloned.1.call-start = ((), (), s32[]{:S(2)}) async-start(), calls=%async_computation.18 | async-start | bytes 2654208 | tf_op jit(solution)/shard_map/reduce_scatter | solution.py:247
  622.3 210.5 %reduce-scatter.21.cloned.1.call-start = ((), (), s32[]{:S(2)}) async-start(), calls=%async_computation.17 | async-start | bytes 2654208 | tf_op jit(solution)/shard_map/reduce_scatter | solution.py:246
  632.2 247.1 %reduce-scatter.19.cloned.1.call-start = ((), (), s32[]{:S(2)}) async-start(), calls=%async_computation.16 | async-start | bytes 2654208 | tf_op jit(solution)/shard_map/reduce_scatter | solution.py:245
  640.3 8.1 copy-start.47
  640.3 277.8 %reduce-scatter.17.cloned.1.call-start = ((), (), s32[]{:S(2)}) async-start(), calls=%async_computation.15 | async-start | bytes 884736 | tf_op jit(solution)/shard_map/reduce_scatter | solution.py:243
  644.2 313.0 %reduce-scatter.13.cloned.1.call-start = ((), (), s32[]{:S(2)}) async-start(), calls=%async_computation.13 | async-start | bytes 884736 | tf_op jit(solution)/shard_map/reduce_scatter | solution.py:241
  648.1 348.0 %reduce-scatter.15.cloned.1.call-start = ((), (), s32[]{:S(2)}) async-start(), calls=%async_computation.14 | async-start | bytes 884736 | tf_op jit(solution)/shard_map/reduce_scatter | solution.py:242
  649.6 9.0 copy-start.46
  658.6 81.9 %copy-start.27 = (f32[2048]{0:T(1024)S(1)}, f32[2048]{0:T(1024)}, u32[]{:S(2)}) copy-start(f32[2048]{0:T(1024)} %copy-done.26) | copy-start | bytes 24580
  658.6 81.9 %copy-start.31 = (f32[768]{0:T(1024)S(1)}, f32[768]{0:T(1024)}, u32[]{:S(2)}) copy-start(f32[768]{0:T(1024)} %param.27) | copy-start | bytes 9220
  658.7 86.1 %copy-start.34 = (f32[768]{0:T(1024)S(1)}, f32[768]{0:T(1024)}, u32[]{:S(2)}) copy-start(f32[768]{0:T(1024)} %get-tuple-element.246) | copy-start | bytes 9220
  770.6 225.4 %copy-start.1 = (bf16[768,768]{1,0:T(8,128)(2,1)S(1)}, bf16[768,768]{1,0:T(8,128)(2,1)}, u32[]{:S(2)}) copy-start(bf16[768,768]{1,0:T(8,128)(2,1)} %param.29) | copy-start | bytes 3538948
  (40 other events, 128.8 us)
Sparse Core Ops, SparseCore 0:
  71.5 123.7 all-reduce.8
  212.6 120.0 all-reduce.10
  358.1 33.1 reduce-scatter.10
  419.0 121.0 all-reduce.12
  560.2 34.0 reduce-scatter.24
  620.4 120.0 all-reduce.14
  744.4 41.5 reduce-scatter.22
  790.3 42.4 reduce-scatter.20
  836.7 42.4 reduce-scatter.18
  883.1 34.9 reduce-scatter.16
  922.2 34.9 reduce-scatter.12
  961.1 34.9 reduce-scatter.14
where the time goes:
time: 1010 us; the launch traced here: 1000 us
  waiting for transfers between devices  677 us (67%)
  matrix products  169 us (17%)
  other arithmetic  56.7 us (6%)
  local copies, waits for them, and re-layouts  50 us (5%)
  blocking collectives  33.6 us (3%)
  between operations  15.8 us (2%)
    psum x1, waiting for transfers between devices, shards(): middle = x_in + lax.psum(attn_part, 'tp').astype(jnp.float32)  124 us
    psum x1, waiting for transfers between devices, shards(): lax.psum(jnp.einsum('tf,df->td', d_pre, w_hidden, preferred_element_type=...  121 us
    psum x1, waiting for transfers between devices, shards(): result = middle + lax.psum(ffn_part, 'tp').astype(jnp.float32)  118 us
    psum x1, waiting for transfers between devices, shards(): lax.psum(d_normed_part.astype(jnp.bfloat16), 'tp').astype(jnp.float32)  62.5 us
    reduce_scatter x1, waiting for transfers between devices, shards(): lax.psum_scatter(d_down, 'dp', scatter_dimension=1, tiled=True)  46.8 us
    reduce_scatter x1, waiting for transfers between devices, shards(): lax.psum_scatter(d_hidden_w, 'dp', scatter_dimension=0, tiled=True)  46.5 us
    reduce_scatter x1, waiting for transfers between devices, shards(): lax.psum_scatter(d_query_w, 'dp', scatter_dimension=0, tiled=True)  39 us
    reduce_scatter x1, waiting for transfers between devices, shards(): lax.psum_scatter(d_key_w, 'dp', scatter_dimension=0, tiled=True)  38.9 us
  transfers between devices with their start and end apart: 12, of which 11 were waited for; matrix products, arithmetic and copies ran while one was open for 13% of the time, Pallas kernels for 0%

commit v1 on v0

v1 whole, which is shorter than its diff:
```python
import functools
import math

import jax
import jax.numpy as jnp
import numpy as np
from jax import lax
from jax.experimental import pallas as pl
from jax.experimental.pallas import tpu as pltpu
from jax.sharding import PartitionSpec as P

MAX_DIST = 128
SEG_ROW = 8
TILE = 128
VMEM = 52 * 2**20

epsilon = 1e-06
logit_scale = 50.0
loss_scale = 128.0
masked_value = -1e30
highest = lax.Precision.HIGHEST
f32 = jnp.float32
bf16 = jnp.bfloat16

NN = (((1,), (0,)), ((), ()))
NT = (((1,), (1,)), ((), ()))
TN = (((0,), (0,)), ((), ()))


def dg(a, b, dims):
    return lax.dot_general(a, b, dims, preferred_element_type=f32)


def bucket_of(offsets, bucket_count, distance):
    half_count = bucket_count // 2
    exact_count = half_count // 2
    far_side = np.where(offsets > 0, half_count, 0)
    magnitude = np.abs(offsets)
    logged = (
        np.log(np.maximum(magnitude, exact_count) / exact_count)
        / math.log(distance / exact_count)
        * (half_count - exact_count)
    )
    far_bucket = np.minimum(exact_count + logged.astype(np.int64), half_count - 1)
    return (far_side + np.where(magnitude < exact_count, magnitude, far_bucket)).astype(np.int32)


def bias_lanes(bucket_count):
    lanes = np.arange(4 * TILE)
    lanes = np.where(lanes >= 2 * TILE, lanes - 4 * TILE, lanes)
    return np.eye(bucket_count, dtype=np.float32)[bucket_of(-lanes, bucket_count, MAX_DIST)].T


def grad_lanes(bucket_count):
    sub = np.arange(8)[:, None]
    lane = np.arange(4 * TILE)[None, :]
    y = (lane - sub) % (4 * TILE)
    y = np.where(y >= 2 * TILE, y - 4 * TILE, y)
    near = bucket_of(-y, bucket_count, MAX_DIST)
    up = np.full((8, TILE), bucket_of(np.array(MAX_DIST), bucket_count, MAX_DIST))
    down = np.full((8, TILE), bucket_of(np.array(-MAX_DIST), bucket_count, MAX_DIST))
    ids = np.concatenate([near, up, down], 1).reshape(-1)
    return np.eye(bucket_count, dtype=np.float32)[ids]


def spread_bias(vec_ref, bias_s, heads):
    for h in range(heads):
        wide = jnp.broadcast_to(vec_ref[0, h : h + 1, :], (TILE, 4 * TILE))
        bias_s[h] = pltpu.roll(wide, 0, 1, stride=1, stride_axis=0)


def with_bias(tile, offset, h, bias_s, vec_ref):
    if offset == 0:
        return tile + bias_s[h, :, 0:TILE]
    if offset == 1:
        return tile + bias_s[h, :, 3 * TILE : 4 * TILE]
    if offset == -1:
        return tile + bias_s[h, :, TILE : 2 * TILE]
    lane = 2 * TILE + 1 if offset > 1 else 2 * TILE - 1
    return tile + vec_ref[0, h : h + 1, lane : lane + 1]


def masks(seg):
    hot = lax.broadcasted_iota(jnp.int32, (16, seg.shape[-1]), 0) == seg
    return (
        jnp.where(hot, 0.0, masked_value).astype(bf16),
        jnp.where(hot, 1.0, 0.0).astype(bf16),
    )


def attn_kernel(heads, hd, a1_ref, w_ref, vec_ref, seg_ref, *rest):
    qkv_ref, lse_ref, ctx_ref, bias_s = rest[-4:]
    length = a1_ref.shape[0]
    blocks = length // TILE

    @pl.when(pl.program_id(1) == 0)
    def _():
        spread_bias(vec_ref, bias_s, heads)

    qkv_ref[0, 0] = dg(w_ref[0], a1_ref[...], NT).astype(bf16)
    q_mask, k_mask = masks(seg_ref[0])
    ones = jnp.ones((16, length), bf16)
    for h in range(heads):
        q_t = jnp.concatenate([qkv_ref[0, 0, h * hd : (h + 1) * hd], q_mask], 0)
        k_t = jnp.concatenate([qkv_ref[0, 0, (heads + h) * hd : (heads + h + 1) * hd], k_mask], 0)
        v_t = jnp.concatenate(
            [qkv_ref[0, 0, (2 * heads + h) * hd : (2 * heads + h + 1) * hd], ones], 0
        )
        scores = dg(k_t.T, q_t, NN)
        columns = []
        tops = []
        for i in range(blocks):
            tiles = [
                with_bias(
                    scores[j * TILE : (j + 1) * TILE, i * TILE : (i + 1) * TILE],
                    j - i,
                    h,
                    bias_s,
                    vec_ref,
                )
                for j in range(blocks)
            ]
            top = jnp.max(functools.reduce(jnp.maximum, tiles), 0, keepdims=True)
            tops.append(top)
            columns.append(jnp.concatenate([jnp.exp(t - top).astype(bf16) for t in tiles], 0))
        mixed = dg(v_t, jnp.concatenate(columns, 1), NN)
        total = mixed[hd : hd + 1]
        lse_ref[0, 0, h : h + 1, :] = jnp.concatenate(tops, 1) + jnp.log(total)
        ctx_ref[0, 0, h * hd : (h + 1) * hd, :] = (mixed[:hd] / total).astype(bf16)


def attention(a1, weights, vecs, segs, first, slots, earlier=None):
    rows, _, length = segs.shape
    width = a1.shape[1]
    heads = vecs.shape[1]
    hd = width // (4 * heads)
    cols = heads * hd
    count = weights.shape[0]
    grid_spec = dict(
        grid=(count, rows),
        in_specs=[
            pl.BlockSpec((length, width), lambda s, r: (r, 0)),
            pl.BlockSpec((1, 3 * cols, width), lambda s, r: (s, 0, 0)),
            pl.BlockSpec((1, heads, 4 * TILE), lambda s, r: (s, 0, 0)),
            pl.BlockSpec((1, 1, length), lambda s, r: (r, 0, 0)),
        ]
        + ([] if earlier is None else [pl.BlockSpec(memory_space=pl.ANY)] * 3),
        out_specs=[
            pl.BlockSpec((1, 1, 3 * cols, length), lambda s, r: (s + first, r, 0, 0)),
            pl.BlockSpec((1, 1, heads, length), lambda s, r: (s + first, r, 0, 0)),
            pl.BlockSpec((1, 1, cols, length), lambda s, r: (s + first, r, 0, 0)),
        ],
    )
    steps = count * rows
    return pl.pallas_call(
        functools.partial(attn_kernel, heads, hd),
        out_shape=[
            jax.ShapeDtypeStruct((slots, rows, 3 * cols, length), bf16),
            jax.ShapeDtypeStruct((slots, rows, heads, length), f32),
            jax.ShapeDtypeStruct((slots, rows, cols, length), bf16),
        ],
        scratch_shapes=[pltpu.VMEM((heads, TILE, 4 * TILE), f32)],
        input_output_aliases={} if earlier is None else {4: 0, 5: 1, 6: 2},
        compiler_params=pltpu.CompilerParams(vmem_limit_bytes=VMEM),
        cost_estimate=pl.CostEstimate(
            flops=steps * 9 * 10**8, bytes_accessed=steps * 2**21, transcendentals=steps * 10**6
        ),
        name="attention",
        **grid_spec,
    )(a1, weights, vecs, segs, *([] if earlier is None else earlier))


def inv_rms(values):
    return lax.rsqrt(jnp.mean(values * values, -1, keepdims=True) + epsilon)


def mid_kernel(x_ref, ctx_ref, w0_ref, w1_ref, gain_ref, mid_ref, a2_ref):
    parts = [
        dg(ctx_ref[k, 0], w0_ref[...] if k == 0 else w1_ref[k - 1], TN).astype(bf16).astype(f32)
        for k in range(ctx_ref.shape[0])
    ]
    mid = x_ref[...].astype(f32) + tree(parts)
    mid_ref[...] = mid
    a2_ref[...] = (mid * inv_rms(mid) * gain_ref[...]).astype(bf16)


def tree(parts):
    while len(parts) > 1:
        parts = [parts[i] + parts[i + 1] for i in range(0, len(parts), 2)]
    return parts[0]


def middle(x, ctx, own_a, far_a, gain):
    slots, rows, cols, length = ctx.shape
    width = x.shape[1]
    return pl.pallas_call(
        mid_kernel,
        grid=(rows,),
        in_specs=[
            pl.BlockSpec((length, width), lambda r: (r, 0)),
            pl.BlockSpec((slots, 1, cols, length), lambda r: (0, r, 0, 0)),
            pl.BlockSpec((cols, width), lambda r: (3, 0)),
            pl.BlockSpec((slots - 1, cols, width), lambda r: (0, 3, 0)),
            pl.BlockSpec((1, width), lambda r: (0, 0)),
        ],
        out_specs=[pl.BlockSpec((length, width), lambda r: (r, 0))] * 2,
        out_shape=[
            jax.ShapeDtypeStruct(x.shape, f32),
            jax.ShapeDtypeStruct(x.shape, bf16),
        ],
        compiler_params=pltpu.CompilerParams(vmem_limit_bytes=VMEM),
        name="middle",
    )(x, ctx, own_a, far_a, gain)


GELU_A = math.sqrt(2.0 / math.pi)
GELU_B = 0.044715


def gelu_pair(v):
    square = v * v
    t = jnp.tanh(GELU_A * v * (1.0 + GELU_B * square))
    half = 0.5 * (1.0 + t)
    slope = half + 0.5 * v * (1.0 - t * t) * (GELU_A * (1.0 + 3.0 * GELU_B * square))
    return v * half, slope


def ffn_own_kernel(a2_ref, b_ref, c_ref, part_ref, hid_ref, slope_ref):
    hidden, slope = gelu_pair(dg(a2_ref[...], b_ref[...], NN))
    hidden = hidden.astype(bf16)
    hid_ref[...] = hidden
    slope_ref[...] = slope.astype(bf16)
    part_ref[...] = dg(hidden, c_ref[...], NN).astype(bf16)


def ffn_own(a2, own_b, own_c, rows):
    tokens, width = a2.shape
    length = tokens // rows
    units = own_b.shape[1]
    return pl.pallas_call(
        ffn_own_kernel,
        grid=(rows,),
        in_specs=[
            pl.BlockSpec((length, width), lambda r: (r, 0)),
            pl.BlockSpec((width, units), lambda r: (0, 0)),
            pl.BlockSpec((units, width), lambda r: (0, 0)),
        ],
        out_specs=[
            pl.BlockSpec((length, width), lambda r: (r, 0)),
            pl.BlockSpec((length, units), lambda r: (r, 0)),
            pl.BlockSpec((length, units), lambda r: (r, 0)),
        ],
        out_shape=[
            jax.ShapeDtypeStruct((tokens, width), bf16),
            jax.ShapeDtypeStruct((tokens, units), bf16),
            jax.ShapeDtypeStruct((tokens, units), bf16),
        ],
        compiler_params=pltpu.CompilerParams(vmem_limit_bytes=VMEM),
        name="ffn_own",
    )(a2, own_b, own_c)


def ffn_far_kernel(
    row_ref,
    a2_ref,
    mid_ref,
    part_ref,
    own_slope_ref,
    b_ref,
    c_ref,
    gain_ref,
    seg_ref,
    out_ref,
    res_ref,
    pool_ref,
    slope_ref,
):
    mine = pl.program_id(0) == row_ref[0]
    parts = [part_ref[...].astype(f32)]
    for k in range(b_ref.shape[0]):
        hidden, slope = gelu_pair(dg(a2_ref[...], b_ref[k], NN))

        @pl.when(mine)
        def _():
            slope_ref[k + 1] = slope.astype(bf16)

        parts.append(dg(hidden.astype(bf16), c_ref[k], NN).astype(bf16).astype(f32))

    @pl.when(mine)
    def _():
        slope_ref[0] = own_slope_ref[...]

    res = mid_ref[...] + tree(parts)
    res_ref[...] = res
    final = (res * inv_rms(res) * gain_ref[...]).astype(bf16)
    out_ref[...] = final
    seg = seg_ref[0]
    hot = lax.broadcasted_iota(jnp.int32, (SEG_ROW, seg.shape[-1]), 0) == seg
    member = jnp.where(hot, 1.0, 0.0)
    pool_ref[...] = dg(member.astype(bf16), final, NN) / jnp.sum(member, 1, keepdims=True)


def ffn_far(row, a2, mid, part, own_slope, far_b, far_c, gain, segs):
    rows, _, length = segs.shape
    tokens, width = a2.shape
    others, _, units = far_b.shape
    by_row = lambda r, row: (r, 0)
    whole3 = lambda r, row: (0, 0, 0)
    return pl.pallas_call(
        ffn_far_kernel,
        grid_spec=pltpu.PrefetchScalarGridSpec(
            num_scalar_prefetch=1,
            grid=(rows,),
            in_specs=[
                pl.BlockSpec((length, width), by_row),
                pl.BlockSpec((length, width), by_row),
                pl.BlockSpec((length, width), by_row),
                pl.BlockSpec((length, units), by_row),
                pl.BlockSpec((others, width, units), whole3),
                pl.BlockSpec((others, units, width), whole3),
                pl.BlockSpec((1, width), lambda r, row: (0, 0)),
                pl.BlockSpec((1, 1, length), lambda r, row: (r, 0, 0)),
            ],
            out_specs=[
                pl.BlockSpec((length, width), by_row),
                pl.BlockSpec((length, width), by_row),
                pl.BlockSpec((SEG_ROW, width), by_row),
                pl.BlockSpec((others + 1, length, units), whole3),
            ],
        ),
        out_shape=[
            jax.ShapeDtypeStruct((tokens, width), bf16),
            jax.ShapeDtypeStruct((tokens, width), f32),
            jax.ShapeDtypeStruct((rows * SEG_ROW, width), f32),
            jax.ShapeDtypeStruct((others + 1, length, units), bf16),
        ],
        compiler_params=pltpu.CompilerParams(vmem_limit_bytes=VMEM),
        name="ffn_far",
    )(row, a2, mid, part, own_slope, far_b, far_c, gain, segs)


def loss_math(pooled, project, pair_col, pair_row, gain):
    slots = pooled.shape[0]
    projected = dg(pooled, project, NN)
    inv_norm = lax.rsqrt(jnp.sum(projected * projected, -1, keepdims=True) + epsilon)
    unit = projected * inv_norm
    embedded = unit.astype(bf16)
    similar = logit_scale * dg(embedded, embedded, NT)
    rows = lax.broadcasted_iota(jnp.int32, (slots, slots), 0)
    columns = lax.broadcasted_iota(jnp.int32, (slots, slots), 1)
    same = rows == columns
    similar = jnp.where(same, masked_value, similar)
    partner = jnp.where((pair_col == pair_row) & jnp.logical_not(same), 2.0, 0.0)

    def total(axis):
        top = jnp.max(similar, axis, keepdims=True)
        return top + jnp.log(jnp.sum(jnp.exp(similar - top), axis, keepdims=True))

    both = jnp.exp(similar - total(1)) + jnp.exp(similar - total(0)) - partner
    high = both.astype(bf16)
    low = (both - high.astype(f32)).astype(bf16)
    d_unit = (loss_scale * logit_scale) * (dg(high, embedded, NN) + dg(low, embedded, NN))
    d_proj = inv_norm * (d_unit - unit * jnp.sum(d_unit * unit, -1, keepdims=True))
    d_proj = d_proj.astype(bf16)
    d_pooled = dg(d_proj, project, NT)
    d_gain = jnp.sum(d_pooled * pooled.astype(f32), 0, keepdims=True) / gain
    return d_proj, d_pooled, d_gain


def loss_kernel(
    pooled_ref, cols_ref, project_ref, pc_ref, pr_ref, gain_ref, dpool_ref, dproj_ref, dgain_ref
):
    d_proj, d_pooled, d_gain = loss_math(
        pooled_ref[...], project_ref[...], pc_ref[...], pr_ref[...], gain_ref[...]
    )
    dpool_ref[...] = d_pooled
    dproj_ref[...] = dg(cols_ref[...], d_proj, TN)
    dgain_ref[...] = d_gain


def loss_head(pooled, own_cols, project, pairs, gain):
    slots, width = pooled.shape
    pair_col = pairs[:, None]
    pair_row = pairs[None, :]
    if slots > 512:
        d_proj, d_pooled, d_gain = loss_math(pooled, project, pair_col, pair_row, gain)
        return d_pooled, dg(own_cols, d_proj, TN), d_gain
    return pl.pallas_call(
        loss_kernel,
        out_shape=[
            jax.ShapeDtypeStruct((slots, width), f32),
            jax.ShapeDtypeStruct((own_cols.shape[1], project.shape[1]), f32),
            jax.ShapeDtypeStruct((1, width), f32),
        ],
        compiler_params=pltpu.CompilerParams(vmem_limit_bytes=VMEM),
        name="loss_head",
    )(pooled, own_cols, project, pair_col, pair_row, gain)


def d_result_of(res, seg, d_pool, gain):
    hot = lax.broadcasted_iota(jnp.int32, (SEG_ROW, seg.shape[-1]), 0) == seg
    member = jnp.where(hot, 1.0, 0.0)
    per_token = d_pool / jnp.sum(member, 1, keepdims=True)
    high = per_token.astype(bf16)
    low = (per_token - high.astype(f32)).astype(bf16)
    twice = jnp.concatenate([member, member], 0).astype(bf16)
    d_final = dg(twice, jnp.concatenate([high, low], 0), TN)
    scale = inv_rms(res)
    unit = res * scale
    weighted = d_final * gain
    return scale * (weighted - unit * jnp.mean(weighted * unit, -1, keepdims=True))


def ffn_back_kernel(
    row_ref,
    res_ref,
    mid_ref,
    seg_ref,
    dpool_ref,
    gain_end_ref,
    gain_ref,
    slope_ref,
    b_ref,
    c_ref,
    wo_ref,
    dmid_ref,
    dattn_ref,
    dctx_ref,
    dgain_ref,
    dres_s,
    low_s,
    sum_s,
):
    k = pl.program_id(0)

    @pl.when(k == 0)
    def _():
        d_res = d_result_of(res_ref[...], seg_ref[0], dpool_ref[...], gain_end_ref[...])
        dres_s[...] = d_res
        low_s[...] = d_res.astype(bf16)

    d_pre = (dg(low_s[...], c_ref[0], NT) * slope_ref[0].astype(f32)).astype(bf16)
    part = dg(d_pre, b_ref[0], NT)

    @pl.when(k == 0)
    def _():
        sum_s[...] = part

    @pl.when(k > 0)
    def _():
        sum_s[...] += part

    @pl.when(k == pl.num_programs(0) - 1)
    def _():
        mid = mid_ref[...]
        scale = inv_rms(mid)
        unit = mid * scale
        grad = sum_s[...]
        weighted = grad * gain_ref[...]
        d_mid = dres_s[...] + scale * (weighted - unit * jnp.mean(weighted * unit, -1, keepdims=True))
        dgain_ref[...] = jnp.sum(grad * unit, 0, keepdims=True)
        dmid_ref[...] = d_mid
        low = d_mid.astype(bf16)
        dattn_ref[...] = low
        for s in range(wo_ref.shape[0]):
            dctx_ref[s] = dg(wo_ref[s], low, NT).astype(bf16)


def ffn_back(row, res, mid, segs, d_pool, gain_end, gain, slope, all_a, all_b, all_c):
    rows, _, length = segs.shape
    tokens, width = res.shape
    slots, _, units = all_b.shape
    cols = width // 4
    own = lambda k, row: (row[0], 0)
    slot = lambda k, row: (k, 0, 0)
    fixed = lambda k, row: (0, 0)
    return pl.pallas_call(
        ffn_back_kernel,
        grid_spec=pltpu.PrefetchScalarGridSpec(
            num_scalar_prefetch=1,
            grid=(slots,),
            in_specs=[
                pl.BlockSpec((length, width), own),
                pl.BlockSpec((length, width), own),
                pl.BlockSpec((1, 1, length), lambda k, row: (row[0], 0, 0)),
                pl.BlockSpec((SEG_ROW, width), own),
                pl.BlockSpec((1, width), fixed),
                pl.BlockSpec((1, width), fixed),
                pl.BlockSpec((1, length, units), slot),
                pl.BlockSpec((1, width, units), slot),
                pl.BlockSpec((1, units, width), slot),
                pl.BlockSpec((slots, cols, width), lambda k, row: (0, 3, 0)),
            ],
            out_specs=[
                pl.BlockSpec((length, width), fixed),
                pl.BlockSpec((length, width), fixed),
                pl.BlockSpec((slots, cols, length), lambda k, row: (0, 0, 0)),
                pl.BlockSpec((1, width), fixed),
            ],
            scratch_shapes=[
                pltpu.VMEM((length, width), f32),
                pltpu.VMEM((length, width), bf16),
                pltpu.VMEM((length, width), f32),
            ],
        ),
        out_shape=[
            jax.ShapeDtypeStruct((length, width), f32),
            jax.ShapeDtypeStruct((length, width), bf16),
            jax.ShapeDtypeStruct((slots, cols, length), bf16),
            jax.ShapeDtypeStruct((1, width), f32),
        ],
        compiler_params=pltpu.CompilerParams(vmem_limit_bytes=VMEM),
        name="ffn_back",
    )(row, res, mid, segs, d_pool, gain_end, gain, slope, all_b, all_c, all_a)


def fold(tile):
    lanes = tile.shape[1]
    total = tile[0:8]
    for b in range(1, TILE // 8):
        total = total + pltpu.roll(tile[8 * b : 8 * b + 8], lanes - 8 * b, 1)
    return total


def attn_back_kernel(
    heads,
    hd,
    row_ref,
    qkv_ref,
    lse_ref,
    ctx_ref,
    dctx_ref,
    vec_ref,
    seg_ref,
    w_ref,
    x_ref,
    dmid_ref,
    gain_ref,
    dqkv_ref,
    fold_ref,
    dtok_ref,
    dgain_ref,
    bias_s,
    sum_s,
):
    slot = pl.program_id(0)
    length = qkv_ref.shape[-1]
    blocks = length // TILE
    spread_bias(vec_ref, bias_s, heads)
    q_mask, k_mask = masks(seg_ref[0])
    for h in range(heads):
        q_low = qkv_ref[0, 0, h * hd : (h + 1) * hd]
        k_low = qkv_ref[0, 0, (heads + h) * hd : (heads + h + 1) * hd]
        v_low = qkv_ref[0, 0, (2 * heads + h) * hd : (2 * heads + h + 1) * hd]
        dc = dctx_ref[0, h * hd : (h + 1) * hd]
        c = ctx_ref[0, 0, h * hd : (h + 1) * hd]
        delta = jnp.sum(dc.astype(f32) * c.astype(f32), 0, keepdims=True)
        lse = lse_ref[0, 0, h : h + 1]
        scores = dg(
            jnp.concatenate([k_low, k_mask], 0).T, jnp.concatenate([q_low, q_mask], 0), NN
        )
        d_probs = dg(v_low.T, dc, NN)
        probs_cols = []
        score_cols = []
        near = [None, None, None]
        far = [None, None]
        for i in range(blocks):
            at = slice(i * TILE, (i + 1) * TILE)
            probs = []
            grads = []
            for j in range(blocks):
                to = slice(j * TILE, (j + 1) * TILE)
                tile = with_bias(scores[to, at], j - i, h, bias_s, vec_ref)
                prob = jnp.exp(tile - lse[:, at])
                grad = prob * (d_probs[to, at] - delta[:, at])
                probs.append(prob.astype(bf16))
                grads.append(grad.astype(bf16))
                if abs(j - i) <= 1:
                    old = near[j - i + 1]
                    near[j - i + 1] = grad if old is None else old + grad
                else:
                    old = far[int(j < i)]
                    far[int(j < i)] = grad if old is None else old + grad
            probs_cols.append(jnp.concatenate(probs, 0))
            score_cols.append(jnp.concatenate(grads, 0))
        probs = jnp.concatenate(probs_cols, 1)
        grads = jnp.concatenate(score_cols, 1)
        dqkv_ref[0, h * hd : (h + 1) * hd] = dg(k_low, grads, NN).astype(bf16)
        dqkv_ref[0, (heads + h) * hd : (heads + h + 1) * hd] = dg(q_low, grads, NT).astype(bf16)
        dqkv_ref[0, (2 * heads + h) * hd : (2 * heads + h + 1) * hd] = dg(dc, probs, NT).astype(
            bf16
        )
        band = jnp.concatenate([near[1], near[0], jnp.zeros_like(near[0]), near[2]], 1)
        fold_ref[0, h, :, : 4 * TILE] = fold(band)
        for side in range(2):
            total = far[side][0:8]
            for b in range(1, TILE // 8):
                total = total + far[side][8 * b : 8 * b + 8]
            fold_ref[0, h, :, (4 + side) * TILE : (5 + side) * TILE] = total
    part = dg(dqkv_ref[0], w_ref[0], TN)

    @pl.when(slot == 0)
    def _():
        sum_s[...] = part

    @pl.when(slot > 0)
    def _():
        sum_s[...] += part

    @pl.when(slot == pl.num_programs(0) - 1)
    def _():
        x = x_ref[...].astype(f32)
        scale = inv_rms(x)
        unit = x * scale
        grad = sum_s[...]
        weighted = grad * gain_ref[...]
        d_tok = dmid_ref[...] + scale * (weighted - unit * jnp.mean(weighted * unit, -1, keepdims=True))
        dtok_ref[...] = d_tok.astype(bf16)
        dgain_ref[...] = jnp.sum(grad * unit, 0, keepdims=True)


def attn_back(row, qkv, lse, ctx, d_ctx, vecs, segs, all_a, x, d_mid, gain):
    slots, rows, cols3, length = qkv.shape
    heads = lse.shape[2]
    cols = cols3 // 3
    width = x.shape[1]
    own4 = lambda k, row: (k, row[0], 0, 0)
    slot = lambda k, row: (k, 0, 0)
    fixed = lambda k, row: (0, 0)
    return pl.pallas_call(
        functools.partial(attn_back_kernel, heads, cols // heads),
        grid_spec=pltpu.PrefetchScalarGridSpec(
            num_scalar_prefetch=1,
            grid=(slots,),
            in_specs=[
                pl.BlockSpec((1, 1, cols3, length), own4),
                pl.BlockSpec((1, 1, heads, length), own4),
                pl.BlockSpec((1, 1, cols, length), own4),
                pl.BlockSpec((1, cols, length), slot),
                pl.BlockSpec((1, heads, 4 * TILE), slot),
                pl.BlockSpec((1, 1, length), lambda k, row: (row[0], 0, 0)),
                pl.BlockSpec((1, cols3, width), slot),
                pl.BlockSpec((length, width), lambda k, row: (row[0], 0)),
                pl.BlockSpec((length, width), fixed),
                pl.BlockSpec((1, width), fixed),
            ],
            out_specs=[
                pl.BlockSpec((1, cols3, length), slot),
                pl.BlockSpec((1, heads, 8, 6 * TILE), lambda k, row: (k, 0, 0, 0)),
                pl.BlockSpec((length, width), fixed),
                pl.BlockSpec((1, width), fixed),
            ],
            scratch_shapes=[
                pltpu.VMEM((heads, TILE, 4 * TILE), f32),
                pltpu.VMEM((length, width), f32),
            ],
        ),
        out_shape=[
            jax.ShapeDtypeStruct((slots, cols3, length), bf16),
            jax.ShapeDtypeStruct((slots, heads, 8, 6 * TILE), f32),
            jax.ShapeDtypeStruct((length, width), bf16),
            jax.ShapeDtypeStruct((1, width), f32),
        ],
        compiler_params=pltpu.CompilerParams(vmem_limit_bytes=VMEM),
        name="attn_back",
    )(row, qkv, lse, ctx, d_ctx, vecs, segs, all_a, x, d_mid, gain)


def attn_weights_kernel(row_ref, a1_ref, dattn_ref, dqkv_ref, ctx_ref, out_ref, a1_s, dattn_s):
    @pl.when(pl.program_id(0) == 0)
    def _():
        a1_s[...] = a1_ref[...].T
        dattn_s[...] = dattn_ref[...].T

    cols3 = dqkv_ref.shape[1]
    out_ref[0, :, :cols3] = dg(a1_s[...], dqkv_ref[0], NT).astype(bf16)
    out_ref[0, :, cols3:] = dg(dattn_s[...], ctx_ref[0, 0], NT).astype(bf16)


def attn_weights(row, a1, d_attn, d_qkv, ctx):
    slots, cols3, length = d_qkv.shape
    cols = ctx.shape[2]
    width = a1.shape[1]
    return pl.pallas_call(
        attn_weights_kernel,
        grid_spec=pltpu.PrefetchScalarGridSpec(
            num_scalar_prefetch=1,
            grid=(slots,),
            in_specs=[
                pl.BlockSpec((length, width), lambda k, row: (row[0], 0)),
                pl.BlockSpec((length, width), lambda k, row: (0, 0)),
                pl.BlockSpec((1, cols3, length), lambda k, row: (k, 0, 0)),
                pl.BlockSpec((1, 1, cols, length), lambda k, row: (k, row[0], 0, 0)),
            ],
            out_specs=pl.BlockSpec((1, width, cols3 + cols), lambda k, row: (k, 0, 0)),
            scratch_shapes=[pltpu.VMEM((width, length), bf16)] * 2,
        ),
        out_shape=jax.ShapeDtypeStruct((slots, width, cols3 + cols), bf16),
        compiler_params=pltpu.CompilerParams(vmem_limit_bytes=VMEM),
        name="attn_weights",
    )(row, a1, d_attn, d_qkv, ctx)


def ffn_weights_kernel(
    res_ref, seg_ref, dpool_ref, gain_ref, a2_ref, hid_ref, slope_ref, c_ref, out_ref, up_s, down_s
):
    r = pl.program_id(0)
    low = d_result_of(res_ref[...], seg_ref[0], dpool_ref[...], gain_ref[...]).astype(bf16)
    d_pre = (dg(low, c_ref[...], NT) * slope_ref[...].astype(f32)).astype(bf16)
    up = dg(a2_ref[...], d_pre, TN)
    down = dg(low, hid_ref[...], TN)

    @pl.when(r == 0)
    def _():
        up_s[...] = up
        down_s[...] = down

    @pl.when(r > 0)
    def _():
        up_s[...] += up
        down_s[...] += down

    @pl.when(r == pl.num_programs(0) - 1)
    def _():
        out_ref[0] = up_s[...].astype(bf16)
        out_ref[1] = down_s[...].astype(bf16)


def ffn_weights(res, segs, d_pool, gain, a2, hidden, slope, own_c):
    rows, _, length = segs.shape
    width = res.shape[1]
    units = hidden.shape[1]
    by_row = lambda r: (r, 0)
    return pl.pallas_call(
        ffn_weights_kernel,
        grid=(rows,),
        in_specs=[
            pl.BlockSpec((length, width), by_row),
            pl.BlockSpec((1, 1, length), lambda r: (r, 0, 0)),
            pl.BlockSpec((SEG_ROW, width), by_row),
            pl.BlockSpec((1, width), lambda r: (0, 0)),
            pl.BlockSpec((length, width), by_row),
            pl.BlockSpec((length, units), by_row),
            pl.BlockSpec((length, units), by_row),
            pl.BlockSpec((units, width), lambda r: (0, 0)),
        ],
        out_specs=pl.BlockSpec((2, width, units), lambda r: (0, 0, 0)),
        scratch_shapes=[pltpu.VMEM((width, units), f32)] * 2,
        out_shape=jax.ShapeDtypeStruct((2, width, units), bf16),
        compiler_params=pltpu.CompilerParams(vmem_limit_bytes=VMEM),
        name="ffn_weights",
    )(res, segs, d_pool, gain, a2, hidden, slope, own_c)


def shards(
    n_dp,
    n_tp,
    tokens,
    segment_ids,
    pair_order,
    w_query,
    w_key,
    w_value,
    w_out,
    rel_bias,
    gain_attn,
    w_hidden,
    w_down,
    gain_ffn,
    gain_final,
    w_project,
):
    rows, length = segment_ids.shape
    bucket_count, heads = rel_bias.shape
    width = tokens.shape[1]
    dp = lax.axis_index("dp")
    tp = lax.axis_index("tp")
    share = math.gcd(n_dp, 8)
    mates = [[(i, i ^ m) for i in range(n_dp)] for m in range(share)]
    levels = [[(i, i ^ k) for i in range(n_tp)] for k in range(n_tp)]

    def over_dp(value, m):
        return lax.ppermute(value, "dp", mates[m])

    def over_tp(value, k):
        return lax.ppermute(value, "tp", levels[k])

    pack_a = jnp.concatenate([w_query.T, w_key.T, w_value.T, w_out], 0)
    slices = width // share
    low_bits = dp % share

    def fetch(pack):
        mine = lax.dynamic_slice_in_dim(pack, low_bits * slices, slices, 0)
        far = jnp.stack([over_tp(mine, k) for k in range(1, n_tp)])
        if share == 8:
            pieces = {0: far}
            for m in (2, 4, 6):
                pieces[m] = over_dp(far, m)
            for m in (0, 2, 4, 6):
                pieces[m + 1] = over_dp(pieces[m], 1)
        else:
            pieces = {m: over_dp(far, m) if m else far for m in range(share)}
        order = low_bits ^ jnp.arange(share, dtype=jnp.int32)
        stacked = jnp.stack([pieces[m] for m in range(share)])
        sorted_pieces = jnp.take(stacked, order, axis=0)
        return jnp.swapaxes(sorted_pieces, 0, 1).reshape(n_tp - 1, width, pack.shape[1])

    def levels_of(value):
        return jnp.stack([value] + [over_tp(value, k) for k in range(1, n_tp)])

    far_a = fetch(pack_a)
    far_b = fetch(w_hidden)
    far_c = fetch(w_down)
    tables = levels_of(rel_bias)
    vecs = jnp.einsum("kbh,bn->khn", tables, bias_lanes(bucket_count), precision=highest)
    segs = segment_ids[:, None, :]
    row = tp[None].astype(jnp.int32)
    one = gain_attn[None]
    two = gain_ffn[None]
    end = gain_final[None]

    x = tokens.astype(f32)
    a1 = (x * inv_rms(x) * one).astype(bf16)
    state = attention(a1, pack_a[None], vecs[:1], segs, 0, n_tp)
    qkv, lse, ctx = attention(a1, far_a, vecs[1:], segs, 1, n_tp, state)
    mid, a2 = middle(tokens, ctx, pack_a, far_a, two)
    part, hidden, slope = ffn_own(a2, w_hidden, w_down, rows)
    layer_out, res, pooled, slopes = ffn_far(
        row, a2, mid, part, slope, far_b, far_c, end, segs
    )
    pooled_all = lax.all_gather(pooled.astype(bf16), "dp", axis=0, tiled=True)
    block = width // n_dp
    own_cols = lax.dynamic_slice_in_dim(pooled_all, dp * block, block, 1)
    d_pool_all, grad_project, d_gain_end = loss_head(
        pooled_all, own_cols, w_project, pair_order // 2, end
    )
    slots_here = rows * SEG_ROW
    d_pool = lax.dynamic_slice_in_dim(d_pool_all, dp * slots_here, slots_here, 0)
    grad_gain_final = lax.dynamic_slice_in_dim(d_gain_end[0], dp * block, block, 0)

    all_a = jnp.concatenate([pack_a[None], far_a])
    all_b = jnp.concatenate([w_hidden[None], far_b])
    all_c = jnp.concatenate([w_down[None], far_c])
    d_mid, d_attn, d_ctx, d_gain_two = ffn_back(
        row, res, mid, segs, d_pool, end, two, slopes, all_a, all_b, all_c
    )
    d_qkv, folded, d_tok, d_gain_one = attn_back(
        row, qkv, lse, ctx, d_ctx, vecs, segs, all_a, tokens, d_mid, one
    )
    grads_a = attn_weights(row, a1, d_attn, d_qkv, ctx)
    grads_f = ffn_weights(res, segs, d_pool, end, a2, hidden, slope, w_down)

    below, above = [d_tok], [d_tok]
    up = [(i, i + 1) for i in range(n_tp - 1)]
    down = [(i + 1, i) for i in range(n_tp - 1)]
    for _ in range(n_tp - 1):
        below.append(lax.ppermute(below[-1], "tp", up))
        above.append(lax.ppermute(above[-1], "tp", down))
    line = jnp.concatenate(below[::-1] + above[1:])
    d_tokens = lax.dynamic_slice_in_dim(line, (n_tp - 1 - tp) * length, rows * length, 0)
    d_tokens = d_tokens.astype(f32)

    def reduce_dp(value):
        lead = value.shape[:-2]
        parts = value.reshape(lead + (n_dp, block, value.shape[-1]))
        at = len(lead)
        if n_dp != 8:
            summed = lax.psum_scatter(value.astype(f32), "dp", scatter_dimension=at, tiled=True)
            return summed
        parts = parts.reshape(lead + (4, 2, block, value.shape[-1]))
        core = dp % 2
        chip = dp // 2
        keep = lax.dynamic_index_in_dim(parts, core, at + 1, keepdims=False)
        give = lax.dynamic_index_in_dim(parts, 1 - core, at + 1, keepdims=False)
        pair = (keep.astype(f32) + over_dp(give, 1).astype(f32)).astype(bf16)
        took = [lax.dynamic_index_in_dim(pair, chip, at, keepdims=False)]
        for m in (1, 2, 3):
            send = lax.dynamic_index_in_dim(pair, chip ^ m, at, keepdims=False)
            took.append(over_dp(send, 2 * m))
        return tree([t.astype(f32) for t in took])

    own_a = reduce_dp(grads_a).astype(bf16)
    own_f = reduce_dp(grads_f)
    grad_a = tree([own_a[0].astype(f32)] + [over_tp(own_a[k], k).astype(f32) for k in range(1, n_tp)])
    cols = width // 4
    d_rel = jnp.einsum(
        "khn,nb->kbh",
        folded.reshape(n_tp, heads, -1),
        grad_lanes(bucket_count),
        precision=highest,
    )
    d_rel_here = tree([d_rel[0]] + [over_tp(d_rel[k], k) for k in range(1, n_tp)])
    gains = jnp.stack([d_gain_one[0], d_gain_two[0]])
    gains = tree([gains] + [over_tp(gains, k) for k in range(1, n_tp)])
    d_rel_here, gains = lax.psum((d_rel_here, gains), "dp")
    gains = lax.dynamic_slice_in_dim(gains, dp * block, block, 1)
    return (
        layer_out,
        d_tokens,
        grad_a[:, :cols],
        grad_a[:, cols : 2 * cols],
        grad_a[:, 2 * cols : 3 * cols],
        grad_a[:, 3 * cols :].T,
        d_rel_here,
        gains[0],
        own_f[0],
        own_f[1].T,
        gains[1],
        grad_gain_final,
        grad_project,
    )


def solution(mesh):
    placed = (
        P("dp", None),
        P("dp", None),
        P(),
        P(None, "tp"),
        P(None, "tp"),
        P(None, "tp"),
        P("tp", None),
        P(None, "tp"),
        P(),
        P(None, "tp"),
        P("tp", None),
        P(),
        P(),
        P(),
    )
    return jax.shard_map(
        functools.partial(shards, mesh.shape["dp"], mesh.shape["tp"]),
        mesh=mesh,
        in_specs=placed,
        out_specs=(
            P("dp", None),
            P("dp", None),
            P("dp", "tp"),
            P("dp", "tp"),
            P("dp", "tp"),
            P("tp", "dp"),
            P(None, "tp"),
            P("dp"),
            P("dp", "tp"),
            P("tp", "dp"),
            P("dp"),
            P("dp"),
            P("dp", None),
        ),
        check_vma=False,
    )
```

time: 1010 us -> 467 us (0.46)
  waiting for transfers between devices: 677 us -> 100 us
  matrix products: 169 us -> 2.29 us
  Pallas kernels: 0 us -> 157 us
  starting transfers between devices: 0.96 us -> 70.8 us
  local copies, waits for them, and re-layouts: 50 us -> 73.3 us
  other arithmetic: 56.7 us -> 35.4 us
  between operations: 15.8 us -> 1.37 us
  blocking collectives: 33.6 us -> 22.4 us
    psum x4 -> x0, waiting for transfers between devices: 425 us -> none  [the longest x1 124 us: shards(): middle = x_in + lax.psum(attn_part, 'tp').astype(jnp.float32)]
    reduce_scatter x7 -> x0, waiting for transfers between devices: 251 us -> none  [the longest x1 46.8 us: shards(): lax.psum_scatter(d_down, 'dp', scatter_dimension=1, tiled=True)]
    dot_general x55 -> x2, matrix products: 167 us -> 2.29 us  [the longest x1 1.26 us: shards(): jnp.einsum('khn,nb->kbh', folded.reshape(n_tp, heads, -1), grad_lanes(buc...]
    pallas_call x0 -> x10, Pallas kernels: none -> 157 us  [the longest x2 40.3 us: attention(): pl.pallas_call(functools.partial(attn_kernel, heads, hd), out_shape=[jax....]
    ppermute x0 -> x56, waiting for transfers between devices: none -> 100 us  [the longest x29 54 us: over_dp(): return lax.ppermute(value, 'dp', mates[m])]
    ppermute x0 -> x56, starting transfers between devices: none -> 70.8 us  [the longest x21 34.1 us: over_tp(): return lax.ppermute(value, 'tp', levels[k])]
    reduce_sum x11 -> x1, other arithmetic: 24.1 us -> 2.57 us  [inv_rms(): return lax.rsqrt(jnp.mean(values * values, -1, keepdims=True) + epsilon)]
    add x8 -> x4, other arithmetic: 21.1 us -> 0.24 us  [tree(): parts = [parts[i] + parts[i + 1] for i in range(0, len(parts), 2)]]
  transfers between devices with their start and end apart: 12 -> 56, of which waited for: 11 -> 14; matrix products, arithmetic and copies ran while one was open for 13% -> 18% of each run, Pallas kernels for 0% -> 11%
where the time goes in v1:
time: 467 us; the launch traced here: 463 us
  Pallas kernels  157 us (34%)
  waiting for transfers between devices  100 us (21%)
  local copies, waits for them, and re-layouts  73.3 us (16%)
  starting transfers between devices  70.8 us (15%)
  other arithmetic  35.4 us (8%)
  blocking collectives  22.4 us (5%)
    ppermute x29, waiting for transfers between devices, over_dp(): return lax.ppermute(value, 'dp', mates[m])  54 us
    pallas_call x2, Pallas kernels, attention(): pl.pallas_call(functools.partial(attn_kernel, heads, hd), out_shape=[jax....  40.3 us
    pallas_call x1, Pallas kernels, ffn_far(): pl.pallas_call(ffn_far_kernel, grid_spec=pltpu.PrefetchScalarGridSpec(num...  36.4 us
    ppermute x21, starting transfers between devices, over_tp(): return lax.ppermute(value, 'tp', levels[k])  34.1 us
    ppermute x21, waiting for transfers between devices, over_tp(): return lax.ppermute(value, 'tp', levels[k])  32.3 us
    unnamed x74, local copies, waits for them, and re-layouts  28 us
    ppermute x29, starting transfers between devices, over_dp(): return lax.ppermute(value, 'dp', mates[m])  22.6 us
    pallas_call x1, Pallas kernels, attn_back(): pl.pallas_call(functools.partial(attn_back_kernel, heads, cols // heads),...  17.4 us
  transfers between devices with their start and end apart: 56, of which 14 were waited for; matrix products, arithmetic and copies ran while one was open for 18% of the time, Pallas kernels for 11%

profile of v1, /device:TPU:0, one launch (start us, length us, event | category | flops | bytes accessed | tf_op | source)
XLA Modules:
  0.0 462.6 jit_solution(2441019594303991433)
XLA Ops:
  8.9 3.9 collective-permute-start.12
  28.5 4.4 collective-permute-start.14
  35.4 11.0 %attention.2 = (bf16[4,4,576,512]{3,2,1,0:T(8,128)(2,1)}, f32[4,4,3,512]{3,2,1,0:T(4,128)S(1)}, bf16[4,4,192,512]{3,2,1,0:T(8,128)(2,1)}) custom-call(bf16[2048,768]{1,0:T(8,128)(2,1)} %fusion.2.a1_ref, bf16[1,768,768]{2,1,0:T(8,128)(2,1)S(1)} %get-tuple-element.115.w_ref, f32[1,3,512]{2,1,0:T(4,128)S(1)} %slice.79.vec_ref, ...), custom_call_target="tpu_custom_call" | custom-call | flops 3600000000 | bytes 8388608 | tf_op jit(solution)/shard_map/attention/pallas_call | solution.py:155
  60.0 4.8 %collective-permute-done.24 = bf16[96,768]{1,0:T(8,128)(2,1)S(1)} collective-permute-done((bf16[96,768]{1,0:T(8,128)(2,1)S(1)}, bf16[96,768]{1,0:T(8,128)(2,1)S(1)}, u32[]{:S(2)}, u32[]{:S(2)}) %collective-permute-start.24) | collective-permute-done | bytes 147488 | tf_op jit(solution)/shard_map/ppermute | solution.py:786
  72.3 13.8 %collective-permute-done.17 = bf16[3,96,768]{2,1,0:T(8,128)(2,1)} collective-permute-done((bf16[3,96,768]{2,1,0:T(8,128)(2,1)}, bf16[3,96,768]{2,1,0:T(8,128)(2,1)}, u32[]{:S(2)}, u32[]{:S(2)}) %collective-permute-start.17) | collective-permute-done | bytes 442400 | tf_op jit(solution)/shard_map/ppermute | solution.py:783
  90.3 5.8 %collective-permute-done.27 = bf16[3,96,768]{2,1,0:T(8,128)(2,1)S(1)} collective-permute-done((bf16[3,96,768]{2,1,0:T(8,128)(2,1)}, bf16[3,96,768]{2,1,0:T(8,128)(2,1)S(1)}, u32[]{:S(2)}, u32[]{:S(2)}) %collective-permute-start.27) | collective-permute-done | bytes 442400 | tf_op jit(solution)/shard_map/ppermute | solution.py:783
  96.1 4.2 collective-permute-start.21
  106.9 4.8 %gather_fusion = bf16[8,3,96,768]{3,2,1,0:T(8,128)(2,1)} fusion(bf16[8,3,96,768]{3,2,1,0:T(8,128)(2,1)} %bitcast_dynamic-update-slice_fusion.16, s32[1024]{0:T(1024)} %pad_clamp_fusion), kind=kCustom, calls=%fused_computation.clone | custom fusion | bytes 7077920 | tf_op jit(solution)/shard_map/jit(_take)/gather | solution.py:805
  112.3 14.8 %collective-permute-done.29 = bf16[3,96,768]{2,1,0:T(8,128)(2,1)} collective-permute-done((bf16[3,96,768]{2,1,0:T(8,128)(2,1)}, bf16[3,96,768]{2,1,0:T(8,128)(2,1)}, u32[]{:S(2)}, u32[]{:S(2)}) %collective-permute-start.29) | collective-permute-done | bytes 442400 | tf_op jit(solution)/shard_map/ppermute | solution.py:783
  134.7 4.6 %gather_fusion.1 = bf16[8,3,96,768]{3,2,1,0:T(8,128)(2,1)} fusion(bf16[8,3,96,768]{3,2,1,0:T(8,128)(2,1)} %bitcast_dynamic-update-slice_fusion.8, s32[1024]{0:T(1024)} %pad_clamp_fusion), kind=kCustom, calls=%fused_computation.1.clone | custom fusion | bytes 7077920 | tf_op jit(solution)/shard_map/jit(_take)/gather | solution.py:805
  148.3 4.7 %gather_fusion.2 = bf16[8,3,96,768]{3,2,1,0:T(8,128)(2,1)} fusion(bf16[8,3,96,768]{3,2,1,0:T(8,128)(2,1)} %bitcast_dynamic-update-slice_fusion, s32[1024]{0:T(1024)} %pad_clamp_fusion), kind=kCustom, calls=%fused_computation.2.clone | custom fusion | bytes 7077920 | tf_op jit(solution)/shard_map/jit(_take)/gather | solution.py:805
  153.0 4.6 %select_bitcast_fusion = (bf16[3,8,96,768]{3,2,0,1:T(8,128)(2,1)S(1)}, bf16[3,8,96,768]{3,2,0,1:T(8,128)(2,1)S(1)}, bf16[3,8,96,768]{3,2,0,1:T(8,128)(2,1)S(1)}) fusion(bf16[8,3,96,768]{3,2,1,0:T(8,128)(2,1)} %gather_fusion.2, pred[8]{0:T(512)(128)(4,1)} %compare_and_fusion, bf16[8,3,96,768]{3,2,1,0:T(8,128)(2,1)} %gather_fusion.1, ...), kind=kLoop, calls=%fused_computation.13 | loop fusion | flops 5308416 | bytes 21233672 | tf_op jit(solution)/shard_map/transpose | solution.py:806
  159.7 29.3 %attention.3 = (bf16[4,4,576,512]{3,2,1,0:T(8,128)(2,1)}, f32[4,4,3,512]{3,2,1,0:T(4,128)S(1)}, bf16[4,4,192,512]{3,2,1,0:T(8,128)(2,1)}) custom-call(bf16[2048,768]{1,0:T(8,128)(2,1)} %fusion.2.a1_ref, bf16[3,768,768]{2,1,0:T(8,128)(2,1)} %bitcast.168, f32[3,3,512]{2,1,0:T(4,128)S(1)} %copy-done.8, ...), custom_call_target="tpu_custom_call", output_to_operand_aliasing={{0}: (4, {}), {1}: (5, {}), {2}: (6, {})} | custom-call | flops 10800000000 | bytes 25165824 | tf_op jit(solution)/shard_map/attention/pallas_call | solution.py:155
  189.0 9.3 %middle.1 = (f32[2048,768]{1,0:T(8,128)}, bf16[2048,768]{1,0:T(8,128)(2,1)}) custom-call(bf16[2048,768]{1,0:T(8,128)(2,1)} %x_ref.3, bf16[4,4,192,512]{3,2,1,0:T(8,128)(2,1)} %get-tuple-element.43.ctx_ref, bf16[768,768]{1,0:T(8,128)(2,1)S(1)} %get-tuple-element.116.w0_ref, bf16[3,768,768]{2,1,0:T(8,128)(2,1)} %bitcast.169, ...), custom_call_target="tpu_custom_call" | custom-call | tf_op jit(solution)/shard_map/middle/pallas_call | solution.py:196
  198.3 10.9 %ffn_own.1 = (bf16[2048,768]{1,0:T(8,128)(2,1)}, bf16[2048,768]{1,0:T(8,128)(2,1)}, bf16[2048,768]{1,0:T(8,128)(2,1)}) custom-call(bf16[2048,768]{1,0:T(8,128)(2,1)} %get-tuple-element.44.a2_ref, bf16[768,768]{1,0:T(8,128)(2,1)S(1)} %copy-done.1, bf16[768,768]{1,0:T(8,128)(2,1)} %c_ref.3), custom_call_target="tpu_custom_call" | custom-call | tf_op jit(solution)/shard_map/ffn_own/pallas_call | solution.py:240
  213.4 36.4 %ffn_far.1 = (bf16[2048,768]{1,0:T(8,128)(2,1)}, f32[2048,768]{1,0:T(8,128)}, f32[32,768]{1,0:T(8,128)S(1)}, bf16[4,512,768]{2,1,0:T(8,128)(2,1)}) custom-call(s32[1]{0:T(128)} %bitcast.row_ref, bf16[2048,768]{1,0:T(8,128)(2,1)} %get-tuple-element.44.a2_ref, f32[2048,768]{1,0:T(8,128)} %get-tuple-element.45.mid_ref, ...), custom_call_target="tpu_custom_call" | custom-call | tf_op jit(solution)/shard_map/ffn_far/pallas_call | solution.py:309
  249.8 9.8 %all_gather.3.pooled_ref = bf16[256,768]{1,0:T(8,128)(2,1)S(1)} all-gather(bf16[32,768]{1,0:T(8,128)(2,1)S(1)} %convert_element_type.86), channel_id=1, replica_groups=mesh['dp'=8,'tp'=4] {'dp'}, dimensions={0}, use_global_device_ids=true | all-gather | bytes 442368 | tf_op jit(solution)/shard_map/all_gather | solution.py:831
  259.6 4.2 loss_head.1
  263.9 16.9 %ffn_weights.1 = bf16[2,768,768]{2,1,0:T(8,128)(2,1)} custom-call(f32[2048,768]{1,0:T(8,128)} %get-tuple-element.51.res_ref, s32[4,1,512]{2,1,0:T(1,128)S(1)} %broadcast_in_dim.42.seg_ref, f32[32,768]{1,0:T(8,128)S(1)} %constant_dynamic-slice_fusion.4.dpool_ref, f32[1,768]{1,0:T(1,128)S(1)} %broadcast_in_dim.45.gain_ref.gain_end_ref, ...), custom_call_target="tpu_custom_call" | custom-call | tf_op jit(solution)/shard_map/ffn_weights/pallas_call | solution.py:734
  285.4 4.2 pad_maximum_fusion
  292.1 13.9 %ffn_back.1 = (f32[512,768]{1,0:T(8,128)}, bf16[512,768]{1,0:T(8,128)(2,1)S(1)}, bf16[4,192,512]{2,1,0:T(8,128)(2,1)S(1)}, f32[1,768]{1,0:T(1,128)S(1)}) custom-call(s32[1]{0:T(128)} %bitcast.row_ref, f32[2048,768]{1,0:T(8,128)} %get-tuple-element.51.res_ref, f32[2048,768]{1,0:T(8,128)} %get-tuple-element.45.mid_ref, ...), custom_call_target="tpu_custom_call" | custom-call | tf_op jit(solution)/shard_map/ffn_back/pallas_call | solution.py:477
  306.9 17.4 %attn_back.1 = (bf16[4,576,512]{2,1,0:T(8,128)(2,1)}, f32[4,3,8,768]{3,2,1,0:T(8,128)S(1)}, bf16[512,768]{1,0:T(8,128)(2,1)S(1)}, f32[1,768]{1,0:T(1,128)S(1)}) custom-call(s32[1]{0:T(128)} %bitcast.row_ref, bf16[4,4,576,512]{3,2,1,0:T(8,128)(2,1)} %get-tuple-element.49.qkv_ref, f32[4,4,3,512]{3,2,1,0:T(4,128)S(1)} %get-tuple-element.50.lse_ref, ...), custom_call_target="tpu_custom_call" | custom-call | tf_op jit(solution)/shard_map/attn_back/pallas_call | solution.py:630
  328.2 7.8 %attn_weights.1 = bf16[4,768,768]{2,1,0:T(8,128)(2,1)} custom-call(s32[1]{0:T(128)} %bitcast.row_ref, bf16[2048,768]{1,0:T(8,128)(2,1)} %fusion.2.a1_ref, bf16[512,768]{1,0:T(8,128)(2,1)S(1)} %get-tuple-element.58.dattn_ref, bf16[4,576,512]{2,1,0:T(8,128)(2,1)} %get-tuple-element.59.dqkv_ref, bf16[4,4,192,512]{3,2,1,0:T(8,128)(2,1)} %get-tuple-element.43.ctx_ref), custom_call_target="tpu_custom_call" | custom-call | tf_op jit(solution)/shard_map/attn_weights/pallas_call | solution.py:684
  348.5 5.6 %collective-permute-start.47 = (f32[32,3]{0,1:T(4,128)S(1)}, f32[32,3]{0,1:T(4,128)S(1)}, u32[]{:S(2)}, u32[]{:S(2)}) collective-permute-start(f32[32,3]{0,1:T(4,128)S(1)} %bitcast.196), channel_id=1, source_target_pairs={{0,2},{1,3},{2,0},{3,1},{4,6},{5,7},{6,4},{7,5},{8,10},{9,11},{10,... | collective-permute-start | bytes 1160 | tf_op jit(solution)/shard_map/ppermute | solution.py:786
  365.5 12.4 %collective-permute-done.51 = f32[2,768]{1,0:T(2,128)S(1)} collective-permute-done((f32[2,768]{1,0:T(2,128)S(1)}, f32[2,768]{1,0:T(2,128)S(1)}, u32[]{:S(2)}, u32[]{:S(2)}) %collective-permute-start.51) | collective-permute-done | bytes 6176 | tf_op jit(solution)/shard_map/ppermute | solution.py:786
  378.0 12.7 %all-reduce = (f32[32,3]{0,1:T(4,128)}, f32[2,768]{1,0:T(2,128)S(1)}) all-reduce(f32[32,3]{0,1:T(4,128)S(1)} %fusion.11, f32[2,768]{1,0:T(2,128)S(1)} %add_add_fusion), channel_id=1, replica_groups=mesh['dp'=8,'tp'=4] {'dp'}, use_global_device_ids=true, to_apply=%region_1.3 | all-reduce | flops 1632 | bytes 13056 | tf_op jit(solution)/shard_map/psum | solution.py:895
  394.1 4.6 collective-permute-start.35
  398.7 8.3 %collective-permute-done.54 = bf16[2,96,768]{2,1,0:T(8,128)(2,1)S(1)} collective-permute-done((bf16[2,96,768]{2,1,0:T(8,128)(2,1)S(1)}, bf16[2,96,768]{2,1,0:T(8,128)(2,1)S(1)}, u32[]{:S(2)}, u32[]{:S(2)}) %collective-permute-start.54) | collective-permute-done | bytes 294944 | tf_op jit(solution)/shard_map/ppermute | solution.py:783
  408.0 4.2 collective-permute-done.37
  424.0 9.4 %collective-permute-done.38 = bf16[512,768]{1,0:T(8,128)(2,1)S(1)} collective-permute-done((bf16[512,768]{1,0:T(8,128)(2,1)S(1)}, bf16[512,768]{1,0:T(8,128)(2,1)S(1)}, u32[]{:S(2)}, u32[]{:S(2)}) %collective-permute-start.38) | collective-permute-done | bytes 786464 | tf_op jit(solution)/shard_map/ppermute | solution.py:858
  433.5 11.3 %collective-permute-done.42 = bf16[4,96,768]{2,1,0:T(8,128)(2,1)S(1)} collective-permute-done((bf16[4,96,768]{2,1,0:T(8,128)(2,1)S(1)}, bf16[4,96,768]{2,1,0:T(8,128)(2,1)S(1)}, u32[]{:S(2)}, u32[]{:S(2)}) %collective-permute-start.42) | collective-permute-done | bytes 589856 | tf_op jit(solution)/shard_map/ppermute | solution.py:783
  454.2 6.7 %collective-permute-done.44 = bf16[96,768]{1,0:T(8,128)(2,1)S(1)} collective-permute-done((bf16[96,768]{1,0:T(8,128)(2,1)S(1)}, bf16[96,768]{1,0:T(8,128)(2,1)S(1)}, u32[]{:S(2)}, u32[]{:S(2)}) %collective-permute-start.44) | collective-permute-done | bytes 147488 | tf_op jit(solution)/shard_map/ppermute | solution.py:786
  (236 shorter events, 144.7 us)
Async XLA Ops:
  2.8 44.1 %collective-permute-start = (bf16[96,768]{1,0:T(8,128)(2,1)}, bf16[96,768]{1,0:T(8,128)(2,1)}, u32[]{:S(2)}, u32[]{:S(2)}) collective-permute-start(bf16[96,768]{1,0:T(8,128)(2,1)} %constant_dynamic-slice_fusion.8), channel_id=1, source_target_pairs={{0,1},{1,0},{2,3},{3,2},{4,5},{5,4},{6,7},{7,6},{8,9},{9,8},{10,11... | collective-permute-start | bytes 442376 | tf_op jit(solution)/shard_map/ppermute | solution.py:786
  5.9 41.1 %collective-permute-start.1 = (bf16[96,768]{1,0:T(8,128)(2,1)}, bf16[96,768]{1,0:T(8,128)(2,1)}, u32[]{:S(2)}, u32[]{:S(2)}) collective-permute-start(bf16[96,768]{1,0:T(8,128)(2,1)} %constant_dynamic-slice_fusion.8), channel_id=1, source_target_pairs={{0,2},{1,3},{2,0},{3,1},{4,6},{5,7},{6,4},{7,5},{8,10},{9,11},{10,... | collective-permute-start | bytes 442376 | tf_op jit(solution)/shard_map/ppermute | solution.py:786
  8.5 18.8 %collective-permute-start.10 = (f32[32,3]{0,1:T(4,128)}, f32[32,3]{0,1:T(4,128)}, u32[]{:S(2)}, u32[]{:S(2)}) collective-permute-start(f32[32,3]{0,1:T(4,128)} %param.25), channel_id=1, source_target_pairs={{0,1},{1,0},{2,3},{3,2},{4,5},{5,4},{6,7},{7,6},{8,9},{9,8},{10,11... | collective-permute-start | bytes 1160 | tf_op jit(solution)/shard_map/ppermute | solution.py:786
  8.9 19.0 %collective-permute-start.11 = (f32[32,3]{0,1:T(4,128)}, f32[32,3]{0,1:T(4,128)}, u32[]{:S(2)}, u32[]{:S(2)}) collective-permute-start(f32[32,3]{0,1:T(4,128)} %param.25), channel_id=1, source_target_pairs={{0,2},{1,3},{2,0},{3,1},{4,6},{5,7},{6,4},{7,5},{8,10},{9,11},{10,... | collective-permute-start | bytes 1160 | tf_op jit(solution)/shard_map/ppermute | solution.py:786
  8.9 19.6 %collective-permute-start.12 = (f32[32,3]{0,1:T(4,128)}, f32[32,3]{0,1:T(4,128)}, u32[]{:S(2)}, u32[]{:S(2)}) collective-permute-start(f32[32,3]{0,1:T(4,128)} %param.25), channel_id=1, source_target_pairs={{0,3},{1,2},{2,1},{3,0},{4,7},{5,6},{6,5},{7,4},{8,11},{9,10},{10,... | collective-permute-start | bytes 1160 | tf_op jit(solution)/shard_map/ppermute | solution.py:786
  27.2 20.4 %collective-permute-start.2 = (bf16[96,768]{1,0:T(8,128)(2,1)}, bf16[96,768]{1,0:T(8,128)(2,1)S(1)}, u32[]{:S(2)}, u32[]{:S(2)}) collective-permute-start(bf16[96,768]{1,0:T(8,128)(2,1)} %constant_dynamic-slice_fusion.8), channel_id=1, source_target_pairs={{0,3},{1,2},{2,1},{3,0},{4,7},{5,6},{6,5},{7,4},{8,11},{9,10},{10,... | collective-permute-start | bytes 442376 | tf_op jit(solution)/shard_map/ppermute | solution.py:786
  27.9 26.3 %collective-permute-start.13 = (bf16[96,768]{1,0:T(8,128)(2,1)}, bf16[96,768]{1,0:T(8,128)(2,1)S(1)}, u32[]{:S(2)}, u32[]{:S(2)}) collective-permute-start(bf16[96,768]{1,0:T(8,128)(2,1)} %constant_dynamic-slice_fusion.7), channel_id=1, source_target_pairs={{0,1},{1,0},{2,3},{3,2},{4,5},{5,4},{6,7},{7,6},{8,9},{9,8},{10,11... | collective-permute-start | bytes 442376 | tf_op jit(solution)/shard_map/ppermute | solution.py:786
  28.5 25.8 %collective-permute-start.14 = (bf16[96,768]{1,0:T(8,128)(2,1)}, bf16[96,768]{1,0:T(8,128)(2,1)S(1)}, u32[]{:S(2)}, u32[]{:S(2)}) collective-permute-start(bf16[96,768]{1,0:T(8,128)(2,1)} %constant_dynamic-slice_fusion.7), channel_id=1, source_target_pairs={{0,2},{1,3},{2,0},{3,1},{4,6},{5,7},{6,4},{7,5},{8,10},{9,11},{10,... | collective-permute-start | bytes 442376 | tf_op jit(solution)/shard_map/ppermute | solution.py:786
  47.6 17.2 %collective-permute-start.24 = (bf16[96,768]{1,0:T(8,128)(2,1)S(1)}, bf16[96,768]{1,0:T(8,128)(2,1)S(1)}, u32[]{:S(2)}, u32[]{:S(2)}) collective-permute-start(bf16[96,768]{1,0:T(8,128)(2,1)S(1)} %copy-done.19), channel_id=1, source_target_pairs={{0,2},{1,3},{2,0},{3,1},{4,6},{5,7},{6,4},{7,5},{8,10},{9,11},{10,... | collective-permute-start | bytes 442376 | tf_op jit(solution)/shard_map/ppermute | solution.py:786
  58.5 42.5 %collective-permute-start.6 = (bf16[3,96,768]{2,1,0:T(8,128)(2,1)S(1)}, bf16[3,96,768]{2,1,0:T(8,128)(2,1)S(1)}, u32[]{:S(2)}, u32[]{:S(2)}) collective-permute-start(bf16[3,96,768]{2,1,0:T(8,128)(2,1)S(1)} %pad_maximum_fusion.4), channel_id=1, source_target_pairs={{0,16},{4,20},{8,24},{12,28},{16,0},{20,4},{24,8},{28,12},{1,17},{... | collective-permute-start | bytes 1327112 | tf_op jit(solution)/shard_map/ppermute | solution.py:783
  64.8 36.2 %collective-permute-start.8 = (bf16[3,96,768]{2,1,0:T(8,128)(2,1)S(1)}, bf16[3,96,768]{2,1,0:T(8,128)(2,1)S(1)}, u32[]{:S(2)}, u32[]{:S(2)}) collective-permute-start(bf16[3,96,768]{2,1,0:T(8,128)(2,1)S(1)} %pad_maximum_fusion.4), channel_id=1, source_target_pairs={{0,24},{4,28},{8,16},{12,20},{16,8},{20,12},{24,0},{28,4},{1,25},{... | collective-permute-start | bytes 1327112 | tf_op jit(solution)/shard_map/ppermute | solution.py:783
  68.8 17.2 %collective-permute-start.17 = (bf16[3,96,768]{2,1,0:T(8,128)(2,1)}, bf16[3,96,768]{2,1,0:T(8,128)(2,1)}, u32[]{:S(2)}, u32[]{:S(2)}) collective-permute-start(bf16[3,96,768]{2,1,0:T(8,128)(2,1)} %pad_maximum_fusion.5), channel_id=1, source_target_pairs={{0,8},{4,12},{8,0},{12,4},{16,24},{20,28},{24,16},{28,20},{1,9},{5... | collective-permute-start | bytes 1327112 | tf_op jit(solution)/shard_map/ppermute | solution.py:783
  70.2 41.5 %collective-permute-start.19 = (bf16[3,96,768]{2,1,0:T(8,128)(2,1)}, bf16[3,96,768]{2,1,0:T(8,128)(2,1)}, u32[]{:S(2)}, u32[]{:S(2)}) collective-permute-start(bf16[3,96,768]{2,1,0:T(8,128)(2,1)} %pad_maximum_fusion.5), channel_id=1, source_target_pairs={{0,16},{4,20},{8,24},{12,28},{16,0},{20,4},{24,8},{28,12},{1,17},{... | collective-permute-start | bytes 1327112 | tf_op jit(solution)/shard_map/ppermute | solution.py:783
  71.5 18.0 %collective-permute-start.26 = (bf16[3,96,768]{2,1,0:T(8,128)(2,1)}, bf16[3,96,768]{2,1,0:T(8,128)(2,1)S(1)}, u32[]{:S(2)}, u32[]{:S(2)}) collective-permute-start(bf16[3,96,768]{2,1,0:T(8,128)(2,1)} %pad_maximum_fusion.6), channel_id=1, source_target_pairs={{0,4},{4,0},{8,12},{12,8},{16,20},{20,16},{24,28},{28,24},{1,5},{5... | collective-permute-start | bytes 1327112 | tf_op jit(solution)/shard_map/ppermute | solution.py:783
  101.0 26.0 %collective-permute-start.29 = (bf16[3,96,768]{2,1,0:T(8,128)(2,1)}, bf16[3,96,768]{2,1,0:T(8,128)(2,1)}, u32[]{:S(2)}, u32[]{:S(2)}) collective-permute-start(bf16[3,96,768]{2,1,0:T(8,128)(2,1)} %pad_maximum_fusion.6), channel_id=1, source_target_pairs={{0,16},{4,20},{8,24},{12,28},{16,0},{20,4},{24,8},{28,12},{1,17},{... | collective-permute-start | bytes 1327112 | tf_op jit(solution)/shard_map/ppermute | solution.py:783
  103.2 23.9 %collective-permute-start.31 = (bf16[3,96,768]{2,1,0:T(8,128)(2,1)}, bf16[3,96,768]{2,1,0:T(8,128)(2,1)}, u32[]{:S(2)}, u32[]{:S(2)}) collective-permute-start(bf16[3,96,768]{2,1,0:T(8,128)(2,1)} %pad_maximum_fusion.6), channel_id=1, source_target_pairs={{0,24},{4,28},{8,16},{12,20},{16,8},{20,12},{24,0},{28,4},{1,25},{... | collective-permute-start | bytes 1327112 | tf_op jit(solution)/shard_map/ppermute | solution.py:783
  105.3 22.2 %collective-permute-start.18 = (bf16[3,96,768]{2,1,0:T(8,128)(2,1)}, bf16[3,96,768]{2,1,0:T(8,128)(2,1)}, u32[]{:S(2)}, u32[]{:S(2)}) collective-permute-start(bf16[3,96,768]{2,1,0:T(8,128)(2,1)} %collective-permute-done.17), channel_id=1, source_target_pairs={{0,4},{4,0},{8,12},{12,8},{16,20},{20,16},{24,28},{28,24},{1,5},{5... | collective-permute-start | bytes 1327112 | tf_op jit(solution)/shard_map/ppermute | solution.py:783
  111.7 27.6 %collective-permute-start.28 = (bf16[3,96,768]{2,1,0:T(8,128)(2,1)}, bf16[3,96,768]{2,1,0:T(8,128)(2,1)}, u32[]{:S(2)}, u32[]{:S(2)}) collective-permute-start(bf16[3,96,768]{2,1,0:T(8,128)(2,1)} %copy-done.18), channel_id=1, source_target_pairs={{0,4},{4,0},{8,12},{12,8},{16,20},{20,16},{24,28},{28,24},{1,5},{5... | collective-permute-start | bytes 1327112 | tf_op jit(solution)/shard_map/ppermute | solution.py:783
  112.2 19.0 %collective-permute-start.20 = (bf16[3,96,768]{2,1,0:T(8,128)(2,1)}, bf16[3,96,768]{2,1,0:T(8,128)(2,1)S(1)}, u32[]{:S(2)}, u32[]{:S(2)}) collective-permute-start(bf16[3,96,768]{2,1,0:T(8,128)(2,1)} %collective-permute-done.19), channel_id=1, source_target_pairs={{0,4},{4,0},{8,12},{12,8},{16,20},{20,16},{24,28},{28,24},{1,5},{5... | collective-permute-start | bytes 1327112 | tf_op jit(solution)/shard_map/ppermute | solution.py:783
  127.6 19.0 %collective-permute-start.32 = (bf16[3,96,768]{2,1,0:T(8,128)(2,1)}, bf16[3,96,768]{2,1,0:T(8,128)(2,1)}, u32[]{:S(2)}, u32[]{:S(2)}) collective-permute-start(bf16[3,96,768]{2,1,0:T(8,128)(2,1)} %collective-permute-done.31), channel_id=1, source_target_pairs={{0,4},{4,0},{8,12},{12,8},{16,20},{20,16},{24,28},{28,24},{1,5},{5... | collective-permute-start | bytes 1327112 | tf_op jit(solution)/shard_map/ppermute | solution.py:783
  284.9 69.2 %collective-permute-start.52 = (bf16[2,4,96,768]{3,2,0,1:T(8,128)(2,1)}, bf16[2,4,96,768]{3,2,0,1:T(8,128)(2,1)}, u32[]{:S(2)}, u32[]{:S(2)}) collective-permute-start(bf16[2,4,96,768]{3,2,0,1:T(8,128)(2,1)} %bitcast.160), channel_id=1, source_target_pairs={{0,4},{4,0},{8,12},{12,8},{16,20},{20,16},{24,28},{28,24},{1,5},{5... | collective-permute-start | bytes 3538952 | tf_op jit(solution)/shard_map/ppermute | solution.py:783
  324.4 35.8 %collective-permute-start.33 = (bf16[512,768]{1,0:T(8,128)(2,1)S(1)}, bf16[512,768]{1,0:T(8,128)(2,1)}, u32[]{:S(2)}, u32[]{:S(2)}) collective-permute-start(bf16[512,768]{1,0:T(8,128)(2,1)S(1)} %get-tuple-element.57), channel_id=1, source_target_pairs={{0,1},{1,2},{2,3},{4,5},{5,6},{6,7},{8,9},{9,10},{10,11},{12,13},{... | collective-permute-start | bytes 2359304 | tf_op jit(solution)/shard_map/ppermute | solution.py:857
  326.7 64.0 %collective-permute-start.36 = (bf16[512,768]{1,0:T(8,128)(2,1)S(1)}, bf16[512,768]{1,0:T(8,128)(2,1)}, u32[]{:S(2)}, u32[]{:S(2)}) collective-permute-start(bf16[512,768]{1,0:T(8,128)(2,1)S(1)} %get-tuple-element.57), channel_id=1, source_target_pairs={{1,0},{2,1},{3,2},{5,4},{6,5},{7,6},{9,8},{10,9},{11,10},{13,12},{... | collective-permute-start | bytes 2359304 | tf_op jit(solution)/shard_map/ppermute | solution.py:858
  339.3 74.2 %collective-permute-start.39 = (bf16[4,4,96,768]{3,2,1,0:T(8,128)(2,1)}, bf16[4,4,96,768]{3,2,1,0:T(8,128)(2,1)}, u32[]{:S(2)}, u32[]{:S(2)}) collective-permute-start(bf16[4,4,96,768]{3,2,1,0:T(8,128)(2,1)} %dynamic-slice_bitcast_fusion), channel_id=1, source_target_pairs={{0,4},{4,0},{8,12},{12,8},{16,20},{20,16},{24,28},{28,24},{1,5},{5... | collective-permute-start | bytes 7077896 | tf_op jit(solution)/shard_map/ppermute | solution.py:783
  360.2 33.9 %collective-permute-start.34 = (bf16[512,768]{1,0:T(8,128)(2,1)}, bf16[512,768]{1,0:T(8,128)(2,1)}, u32[]{:S(2)}, u32[]{:S(2)}) collective-permute-start(bf16[512,768]{1,0:T(8,128)(2,1)} %collective-permute-done.33), channel_id=1, source_target_pairs={{0,1},{1,2},{2,3},{4,5},{5,6},{6,7},{8,9},{9,10},{10,11},{12,13},{... | collective-permute-start | bytes 2359304 | tf_op jit(solution)/shard_map/ppermute | solution.py:857
  364.0 29.4 %collective-permute-start.53 = (bf16[2,96,768]{2,1,0:T(8,128)(2,1)S(1)}, bf16[2,96,768]{2,1,0:T(8,128)(2,1)S(1)}, u32[]{:S(2)}, u32[]{:S(2)}) collective-permute-start(bf16[2,96,768]{2,1,0:T(8,128)(2,1)S(1)} %get-tuple-element.112), channel_id=1, source_target_pairs={{0,8},{4,12},{8,0},{12,4},{16,24},{20,28},{24,16},{28,20},{1,9},{5... | collective-permute-start | bytes 884744 | tf_op jit(solution)/shard_map/ppermute | solution.py:783
  390.6 21.6 %collective-permute-start.37 = (bf16[512,768]{1,0:T(8,128)(2,1)}, bf16[512,768]{1,0:T(8,128)(2,1)S(1)}, u32[]{:S(2)}, u32[]{:S(2)}) collective-permute-start(bf16[512,768]{1,0:T(8,128)(2,1)} %collective-permute-done.36), channel_id=1, source_target_pairs={{1,0},{2,1},{3,2},{5,4},{6,5},{7,6},{9,8},{10,9},{11,10},{13,12},{... | collective-permute-start | bytes 2359304 | tf_op jit(solution)/shard_map/ppermute | solution.py:858
  394.1 26.2 %collective-permute-start.35 = (bf16[512,768]{1,0:T(8,128)(2,1)}, bf16[512,768]{1,0:T(8,128)(2,1)S(1)}, u32[]{:S(2)}, u32[]{:S(2)}) collective-permute-start(bf16[512,768]{1,0:T(8,128)(2,1)} %collective-permute-done.34), channel_id=1, source_target_pairs={{0,1},{1,2},{2,3},{4,5},{5,6},{6,7},{8,9},{9,10},{10,11},{12,13},{... | collective-permute-start | bytes 2359304 | tf_op jit(solution)/shard_map/ppermute | solution.py:857
  412.2 21.2 %collective-permute-start.38 = (bf16[512,768]{1,0:T(8,128)(2,1)S(1)}, bf16[512,768]{1,0:T(8,128)(2,1)S(1)}, u32[]{:S(2)}, u32[]{:S(2)}) collective-permute-start(bf16[512,768]{1,0:T(8,128)(2,1)S(1)} %collective-permute-done.37), channel_id=1, source_target_pairs={{1,0},{2,1},{3,2},{5,4},{6,5},{7,6},{9,8},{10,9},{11,10},{13,12},{... | collective-permute-start | bytes 2359304 | tf_op jit(solution)/shard_map/ppermute | solution.py:858
  416.7 16.8 %collective-permute-start.40 = (bf16[4,96,768]{2,1,0:T(8,128)(2,1)S(1)}, bf16[4,96,768]{2,1,0:T(8,128)(2,1)S(1)}, u32[]{:S(2)}, u32[]{:S(2)}) collective-permute-start(bf16[4,96,768]{2,1,0:T(8,128)(2,1)S(1)} %get-tuple-element.109), channel_id=1, source_target_pairs={{0,8},{4,12},{8,0},{12,4},{16,24},{20,28},{24,16},{28,20},{1,9},{5... | collective-permute-start | bytes 1769480 | tf_op jit(solution)/shard_map/ppermute | solution.py:783
  416.9 16.6 %collective-permute-start.41 = (bf16[4,96,768]{2,1,0:T(8,128)(2,1)S(1)}, bf16[4,96,768]{2,1,0:T(8,128)(2,1)S(1)}, u32[]{:S(2)}, u32[]{:S(2)}) collective-permute-start(bf16[4,96,768]{2,1,0:T(8,128)(2,1)S(1)} %get-tuple-element.111), channel_id=1, source_target_pairs={{0,16},{4,20},{8,24},{12,28},{16,0},{20,4},{24,8},{28,12},{1,17},{... | collective-permute-start | bytes 1769480 | tf_op jit(solution)/shard_map/ppermute | solution.py:783
  418.4 26.5 %collective-permute-start.42 = (bf16[4,96,768]{2,1,0:T(8,128)(2,1)S(1)}, bf16[4,96,768]{2,1,0:T(8,128)(2,1)S(1)}, u32[]{:S(2)}, u32[]{:S(2)}) collective-permute-start(bf16[4,96,768]{2,1,0:T(8,128)(2,1)S(1)} %get-tuple-element.110), channel_id=1, source_target_pairs={{0,24},{4,28},{8,16},{12,20},{16,8},{20,12},{24,0},{28,4},{1,25},{... | collective-permute-start | bytes 1769480 | tf_op jit(solution)/shard_map/ppermute | solution.py:783
  (47 other events, 576.5 us)
